TPU v7x, 32 devices: a whole 2x2x4 slice. The times are simulated.
32 devices in a mesh: rows: 4 (over y, x), frames: 8 (over z, core).
Axes of the slice: x: 2, y: 2, z: 4, core: 2. Of those that a mesh axis runs over, the one named last changes fastest.
Arguments:
- images: bfloat16 [3072, 64, 192], P('frames', 'rows'), may hold values from -6 to 6
- enc_kernel: bfloat16 [4, 4, 3, 48], replicated, may hold values from -0.875 to 0.875
- emb_weight: bfloat16 [1536, 512], P('rows'), may hold values from -0.15625 to 0.15625
- ln1_gain: float32 [512], replicated, may hold values from 0.1 to 1.9
- qkv_weight: bfloat16 [512, 1536], replicated, may hold values from -0.25 to 0.25
- out_weight: bfloat16 [512, 512], replicated, may hold values from -0.5 to 0.5
- ln2_gain: float32 [512], replicated, may hold values from 0.1 to 1.9
- up_weight: bfloat16 [512, 2048], replicated, may hold values from -0.25 to 0.25
- down_weight: bfloat16 [2048, 512], replicated, may hold values from -0.125 to 0.125
- prior_weight: bfloat16 [512, 1024], replicated, may hold values from -0.25 to 0.25
- film_scale: bfloat16 [512, 48], replicated, may hold values from -0.125 to 0.125
- film_shift: bfloat16 [512, 1536], P(None, 'rows'), may hold values from -0.25 to 0.25
- dec_kernel: bfloat16 [4, 4, 48, 3], replicated, may hold values from -0.4375 to 0.4375
- horizons: int32 [192], P('frames'), may hold values from 5 to 15
- frame_valid: int32 [3072], P('frames'), may hold values 0 or 1
- recon_cot: bfloat16 [3072, 64, 192], P('frames', 'rows'), may hold values from -6 to 6
- logit_cot: bfloat16 [3072, 1024], P('frames'), may hold values from -6 to 6
Outputs:
- rebuilt_images: bfloat16 [3072, 64, 192], P('frames', 'rows')
- image_grad: float32 [3072, 64, 192], P('frames', 'rows')
- enc_kernel_grad: float32 [4, 4, 3, 48], replicated
- emb_weight_grad: float32 [1536, 512], P('rows')
- ln1_gain_grad: float32 [512], replicated
- qkv_weight_grad: float32 [512, 1536], replicated
- out_weight_grad: float32 [512, 512], replicated
- ln2_gain_grad: float32 [512], replicated
- up_weight_grad: float32 [512, 2048], replicated
- down_weight_grad: float32 [2048, 512], replicated
- prior_weight_grad: float32 [512, 1024], replicated
- film_scale_grad: float32 [512, 48], replicated
- film_shift_grad: float32 [512, 1536], P(None, 'rows')
- dec_kernel_grad: float32 [4, 4, 48, 3], replicated
All inputs are finite; a program needn't handle non-finite values. No bound on the sum of `frame_valid` on one device may be relied on, other than what follows from the above.
Results may differ from a plain program's by a relative error of at most 0.035.
Values may be sent and summed in bfloat16 or wider, within the bound.
No kernel may reach another device: no remote copies, remote signals or barrier semaphores. Data moves between devices by JAX's collectives and lax.ppermute only.
A program may use at most 384 MiB of HBM per device.

v0:
```python
import math

import jax
import jax.numpy as jnp
from jax import lax
from jax.sharding import PartitionSpec as P

HEADS = 8


HIGHEST = lax.Precision.HIGHEST


def extended(cells, sides, width):
    for axis, dim in sides:
        count = lax.axis_size(axis)
        ends = count - 1
        head = lax.slice_in_dim(cells, 0, width, axis=dim)
        tail = lax.slice_in_dim(cells, cells.shape[dim] - width, cells.shape[dim], axis=dim)
        cells = jnp.concatenate(
            [
                lax.ppermute(tail, axis, [(i, (i + 1) % count) for i in range(ends)]),
                cells,
                lax.ppermute(head, axis, [((i + 1) % count, i) for i in range(ends)]),
            ],
            axis=dim,
        )
    return cells


def gelu_tanh(value):
    return jax.nn.gelu(value, approximate=True)


def gelu_slope(value):
    return jax.jvp(gelu_tanh, (value,), (jnp.ones_like(value),))[1]


def layer_norm(values, gain):
    center = values - jnp.mean(values, axis=-1, keepdims=True)
    spread = jnp.mean(center * center, axis=-1, keepdims=True)
    return center * lax.rsqrt(spread + 1e-05) * gain


def product(pattern, lhs_array, rhs_array):
    return jnp.einsum(pattern, lhs_array, rhs_array, preferred_element_type=jnp.float32)


def tap_layout(tap_count, image_width, map_width):
    offsets = jnp.arange(tap_count)[:, None, None]
    pixel_cols = jnp.arange(image_width)[None, :, None]
    map_cols = jnp.arange(map_width)[None, None, :]
    return (pixel_cols == 2 * map_cols - 1 + offsets).astype(jnp.float32)


def attend_mask(horizon_part, slot_count):
    positions = jnp.arange(slot_count)
    causal = positions[None, :] <= positions[:, None]
    inside = positions[None, :] <= horizon_part[:, None]
    return causal[None, None, :, :] & inside[:, None, None, :]


def pad_rows(values, before, after):
    return jnp.pad(values, ((0, 0), (before, after), (0, 0)))


def block_forward(
    stream, horizon_part, ln1_gain, qkv_weight, out_weight, ln2_gain, up_weight, down_weight
):
    rollouts = horizon_part.shape[0]
    token_count, model_width = stream.shape
    slot_count = token_count // rollouts
    head_size = model_width // HEADS
    scaling = 1.0 / math.sqrt(head_size)
    normed_in = layer_norm(stream, ln1_gain).astype(jnp.bfloat16)
    joined = product("td,de->te", normed_in, qkv_weight).astype(jnp.bfloat16)
    split_shape = (rollouts, slot_count, HEADS, head_size)
    queries = joined[:, :model_width].reshape(split_shape)
    keys_all = joined[:, model_width : 2 * model_width].reshape(split_shape)
    values_all = joined[:, 2 * model_width :].reshape(split_shape)
    raw_scores = product("rqhd,rkhd->rhqk", queries, keys_all) * scaling
    allowed = attend_mask(horizon_part, slot_count)
    attention = jax.nn.softmax(jnp.where(allowed, raw_scores, -1e30), axis=-1)
    attention_low = attention.astype(jnp.bfloat16)
    context = product("rhqk,rkhd->rqhd", attention_low, values_all)
    context = context.reshape(token_count, model_width).astype(jnp.bfloat16)
    middle = stream + product("td,de->te", context, out_weight)
    normed_mid = layer_norm(middle, ln2_gain).astype(jnp.bfloat16)
    raised = product("td,df->tf", normed_mid, up_weight)
    activated = gelu_tanh(raised).astype(jnp.bfloat16)
    result = middle + product("tf,fd->td", activated, down_weight)
    saved_block = (
        stream,
        normed_in,
        queries,
        keys_all,
        values_all,
        attention,
        attention_low,
        context,
        middle,
        normed_mid,
        raised,
        activated,
    )
    return (result, saved_block)


def block_backward(
    grad_out, saved_block, ln1_gain, qkv_weight, out_weight, ln2_gain, up_weight, down_weight
):
    (
        stream,
        normed_in,
        queries,
        keys_all,
        values_all,
        attention,
        attention_low,
        context,
        middle,
        normed_mid,
        raised,
        activated,
    ) = saved_block
    rollouts, slot_count, head_count, head_size = queries.shape
    token_count = rollouts * slot_count
    scaling = 1.0 / math.sqrt(head_size)
    grad_branch = grad_out.astype(jnp.bfloat16)
    down_grad = product("tf,td->fd", activated, grad_branch)
    grad_hidden = product("td,fd->tf", grad_branch, down_weight)
    grad_raised = (grad_hidden * gelu_slope(raised)).astype(jnp.bfloat16)
    up_grad = product("td,tf->df", normed_mid, grad_raised)
    grad_normed = product("tf,df->td", grad_raised, up_weight)
    norm_back = jax.vjp(layer_norm, middle, ln2_gain)[1]
    grad_through, ln2_grad = norm_back(grad_normed)
    grad_middle = grad_out + grad_through
    grad_attended = grad_middle.astype(jnp.bfloat16)
    out_grad = product("te,td->ed", context, grad_attended)
    grad_context = (
        product("td,ed->te", grad_attended, out_weight).astype(jnp.bfloat16).reshape(queries.shape)
    )
    grad_weights = product("rqhd,rkhd->rhqk", grad_context, values_all)
    grad_values = product("rhqk,rqhd->rkhd", attention_low, grad_context)
    grad_scores = attention * (
        grad_weights - jnp.sum(attention * grad_weights, axis=-1, keepdims=True)
    )
    grad_scores = grad_scores.astype(jnp.bfloat16)
    grad_queries = product("rhqk,rkhd->rqhd", grad_scores, keys_all) * scaling
    grad_keys = product("rhqk,rqhd->rkhd", grad_scores, queries) * scaling
    grad_joined = jnp.concatenate(
        [
            grad_queries.reshape(token_count, -1),
            grad_keys.reshape(token_count, -1),
            grad_values.reshape(token_count, -1),
        ],
        axis=1,
    ).astype(jnp.bfloat16)
    qkv_grad = product("td,te->de", normed_in, grad_joined)
    grad_normed_in = product("te,de->td", grad_joined, qkv_weight)
    norm_back_in = jax.vjp(layer_norm, stream, ln1_gain)[1]
    grad_front, ln1_grad = norm_back_in(grad_normed_in)
    return (grad_middle + grad_front, (ln1_grad, qkv_grad, out_grad, ln2_grad, up_grad, down_grad))


def on_device(
    images,
    enc_kernel,
    emb_weight,
    ln1_gain,
    qkv_weight,
    out_weight,
    ln2_gain,
    up_weight,
    down_weight,
    prior_weight,
    film_scale,
    film_shift,
    dec_kernel,
    horizons,
    frame_valid,
    recon_cot,
    logit_cot,
):
    frame_count, row_count, line_width = images.shape
    tap_count = enc_kernel.shape[0]
    chan_in = enc_kernel.shape[2]
    channels = enc_kernel.shape[3]
    image_width = line_width // chan_in
    map_width = image_width // 2
    map_rows = row_count // 2
    map_line = map_width * channels
    pair_width = 2 * line_width
    layout = tap_layout(tap_count, image_width, map_width)
    enc_mats = jnp.einsum(
        "kwj,hkco->hwcjo", layout, enc_kernel.astype(jnp.float32), precision=HIGHEST
    )
    enc_mats = enc_mats.reshape(tap_count, line_width, map_line).astype(jnp.bfloat16)
    enc_front = jnp.concatenate([enc_mats[0], enc_mats[1]], axis=0)
    enc_back = jnp.concatenate([enc_mats[2], enc_mats[3]], axis=0)
    dec_mats = jnp.einsum(
        "kwj,hkoc->hjowc", layout, dec_kernel.astype(jnp.float32), precision=HIGHEST
    )
    dec_mats = dec_mats.reshape(tap_count, map_line, line_width).astype(jnp.bfloat16)
    blank = jnp.zeros((map_line, line_width), jnp.bfloat16)
    dec_table = jnp.concatenate(
        [dec_mats[3], blank, dec_mats[1], dec_mats[2], blank, dec_mats[0]], axis=1
    )
    roll_count = horizons.shape[0]
    slot_count = frame_count // roll_count
    positions = jnp.arange(slot_count)
    live_mask = (positions[None, :] <= horizons[:, None]).reshape(frame_count) & (frame_valid > 0)
    padded = extended(images, (("rows", 1),), 1)
    pairs = padded.reshape(frame_count, map_rows + 1, pair_width)
    front_all = product("tmw,wz->tmz", pairs, enc_front)
    back_all = product("tmw,wz->tmz", pairs, enc_back)
    encoded = front_all[:, :-1] + back_all[:, 1:]
    features = gelu_tanh(encoded).astype(jnp.bfloat16)
    chan_fold = (jnp.arange(map_line)[:, None] % channels == jnp.arange(channels)[None, :]).astype(
        jnp.bfloat16
    )
    profile = (product("tmz,zo->tmo", features, chan_fold) * (1.0 / map_width)).astype(jnp.bfloat16)
    profile = profile.reshape(frame_count, map_rows * channels)
    embed_part = product("tp,pd->td", profile, emb_weight)
    stream_in = lax.psum(embed_part.astype(jnp.bfloat16), "rows").astype(jnp.float32)
    stream_out, saved_block = block_forward(
        stream_in, horizons, ln1_gain, qkv_weight, out_weight, ln2_gain, up_weight, down_weight
    )
    state_part = stream_out.astype(jnp.bfloat16)
    scale_rows = product("td,do->to", state_part, film_scale)
    shift_rows = product("td,dp->tp", state_part, film_shift)
    scale_wide = jnp.tile(scale_rows, (1, map_width))
    shift_wide = jnp.tile(shift_rows.reshape(frame_count, map_rows, channels), (1, 1, map_width))
    modulated = features * (1.0 + scale_wide[:, None, :]) + shift_wide
    decoded = gelu_tanh(modulated).astype(jnp.bfloat16)
    dec_padded = extended(decoded, (("rows", 1),), 1)
    dec_out = product("tmz,zw->tmw", dec_padded, dec_table)
    rebuilt = (
        dec_out[:, :-2, 0:pair_width]
        + dec_out[:, 1:-1, pair_width : 2 * pair_width]
        + dec_out[:, 2:, 2 * pair_width :]
    )
    rebuilt = rebuilt.reshape(frame_count, row_count, line_width)
    grad_rebuilt = jnp.where(live_mask[:, None, None], recon_cot, jnp.zeros_like(recon_cot))
    grad_pairs = grad_rebuilt.reshape(frame_count, map_rows, pair_width)
    grad_spread = jnp.concatenate(
        [pad_rows(grad_pairs, 0, 2), pad_rows(grad_pairs, 1, 1), pad_rows(grad_pairs, 2, 0)], axis=2
    )
    dec_cov = product("tmz,tmw->zw", dec_padded, grad_spread)
    dec_taps = jnp.stack(
        [
            dec_cov[:, 2 * pair_width + line_width :],
            dec_cov[:, pair_width : pair_width + line_width],
            dec_cov[:, pair_width + line_width : 2 * pair_width],
            dec_cov[:, 0:line_width],
        ]
    )
    dec_kernel_grad = jnp.einsum(
        "kwj,hjowc->hkoc",
        layout,
        dec_taps.reshape(tap_count, map_width, channels, image_width, chan_in),
        precision=HIGHEST,
    )
    grad_prev = product("tmw,zw->tmz", grad_pairs, dec_table[:, 0:pair_width])
    grad_center = product("tmw,zw->tmz", grad_pairs, dec_table[:, pair_width : 2 * pair_width])
    grad_next = product("tmw,zw->tmz", grad_pairs, dec_table[:, 2 * pair_width :])
    grad_dec_pad = (
        pad_rows(grad_prev, 0, 2) + pad_rows(grad_center, 1, 1) + pad_rows(grad_next, 2, 0)
    )
    rim_rows = jnp.stack([grad_dec_pad[:, 0], grad_dec_pad[:, -1]], axis=1)
    returned = extended(rim_rows.astype(jnp.bfloat16), (("rows", 1),), 1).astype(rim_rows.dtype)
    grad_decoded = grad_dec_pad[:, 1:-1]
    grad_decoded = grad_decoded.at[:, 0].add(returned[:, 0]).at[:, -1].add(returned[:, 3])
    grad_modulated = (grad_decoded * gelu_slope(modulated)).astype(jnp.bfloat16)
    scale_grad_rows = product("tmz,tmz->tz", grad_modulated, features)
    grad_scale = jnp.sum(scale_grad_rows.reshape(frame_count, map_width, channels), axis=1).astype(
        jnp.bfloat16
    )
    grad_shift = product("tmz,zo->tmo", grad_modulated, chan_fold).reshape(
        frame_count, map_rows * channels
    )
    grad_shift = grad_shift.astype(jnp.bfloat16)
    film_scale_grad = product("td,to->do", state_part, grad_scale)
    film_shift_grad = product("td,tp->dp", state_part, grad_shift)
    grad_film = product("to,do->td", grad_scale, film_scale) + product(
        "tp,dp->td", grad_shift, film_shift
    )
    grad_film_part = lax.psum(grad_film.astype(jnp.bfloat16), "rows").astype(jnp.float32)
    grad_logits = jnp.where(live_mask[:, None], logit_cot, jnp.zeros_like(logit_cot))
    prior_grad = product("td,tc->dc", state_part, grad_logits)
    grad_stream = grad_film_part + product("tc,dc->td", grad_logits, prior_weight)
    grad_embed, block_grads = block_backward(
        grad_stream, saved_block, ln1_gain, qkv_weight, out_weight, ln2_gain, up_weight, down_weight
    )
    ln1_grad, qkv_grad, out_grad, ln2_grad, up_grad, down_grad = block_grads
    grad_embed_low = grad_embed.astype(jnp.bfloat16)
    emb_weight_grad = product("tp,td->pd", profile, grad_embed_low)
    grad_profile = product("td,pd->tp", grad_embed_low, emb_weight) * (1.0 / map_width)
    grad_profile = grad_profile.reshape(frame_count, map_rows, channels)
    grad_features = grad_modulated * (1.0 + scale_wide[:, None, :]) + jnp.tile(
        grad_profile, (1, 1, map_width)
    )
    grad_encoded = (grad_features * gelu_slope(encoded)).astype(jnp.bfloat16)
    tap_front = product("tmw,tmz->wz", pairs[:, :-1], grad_encoded)
    tap_back = product("tmw,tmz->wz", pairs[:, 1:], grad_encoded)
    enc_taps = jnp.concatenate(
        [tap_front.reshape(2, line_width, map_line), tap_back.reshape(2, line_width, map_line)],
        axis=0,
    )
    enc_kernel_grad = jnp.einsum(
        "kwj,hwcjo->hkco",
        layout,
        enc_taps.reshape(tap_count, image_width, chan_in, map_width, channels),
        precision=HIGHEST,
    )
    grad_first = product("tmz,wz->tmw", grad_encoded, enc_front)
    grad_second = product("tmz,wz->tmw", grad_encoded, enc_back)
    grad_padded = (pad_rows(grad_first, 0, 1) + pad_rows(grad_second, 1, 0)).reshape(
        frame_count, row_count + 2, line_width
    )
    image_rim_rows = jnp.stack([grad_padded[:, 0], grad_padded[:, -1]], axis=1)
    image_returned = extended(image_rim_rows.astype(jnp.bfloat16), (("rows", 1),), 1).astype(
        image_rim_rows.dtype
    )
    image_grad = grad_padded[:, 1:-1]
    image_grad = image_grad.at[:, 0].add(image_returned[:, 0]).at[:, -1].add(image_returned[:, 3])
    (
        emb_weight_grad,
        film_shift_grad,
        ln1_grad,
        qkv_grad,
        out_grad,
        ln2_grad,
        up_grad,
        down_grad,
        prior_grad,
    ) = (
        lax.psum(emb_weight_grad.astype(jnp.bfloat16), "frames").astype(jnp.float32),
        lax.psum(film_shift_grad.astype(jnp.bfloat16), "frames").astype(jnp.float32),
        lax.psum(ln1_grad.astype(jnp.bfloat16), "frames").astype(jnp.float32),
        lax.psum(qkv_grad.astype(jnp.bfloat16), "frames").astype(jnp.float32),
        lax.psum(out_grad.astype(jnp.bfloat16), "frames").astype(jnp.float32),
        lax.psum(ln2_grad.astype(jnp.bfloat16), "frames").astype(jnp.float32),
        lax.psum(up_grad.astype(jnp.bfloat16), "frames").astype(jnp.float32),
        lax.psum(down_grad.astype(jnp.bfloat16), "frames").astype(jnp.float32),
        lax.psum(prior_grad.astype(jnp.bfloat16), "frames").astype(jnp.float32),
    )
    enc_kernel_grad, dec_kernel_grad, film_scale_grad = lax.psum(
        (enc_kernel_grad, dec_kernel_grad, film_scale_grad), ("rows", "frames")
    )
    return (
        rebuilt.astype(jnp.bfloat16),
        image_grad,
        enc_kernel_grad,
        emb_weight_grad,
        ln1_grad,
        qkv_grad,
        out_grad,
        ln2_grad,
        up_grad,
        down_grad,
        prior_grad,
        film_scale_grad,
        film_shift_grad,
        dec_kernel_grad,
    )


def solution(mesh):
    return jax.shard_map(
        on_device,
        mesh=mesh,
        in_specs=(
            P("frames", "rows", None),
            P(),
            P("rows", None),
            P(),
            P(),
            P(),
            P(),
            P(),
            P(),
            P(),
            P(),
            P(None, "rows"),
            P(),
            P("frames"),
            P("frames"),
            P("frames", "rows", None),
            P("frames", None),
        ),
        out_specs=(
            P("frames", "rows", None),
            P("frames", "rows", None),
            P(),
            P("rows", None),
            P(),
            P(),
            P(),
            P(),
            P(),
            P(),
            P(),
            P(),
            P(None, "rows"),
            P(),
        ),
        check_vma=False,
    )
```

profile of v0, /device:TPU:0, one launch (start us, length us, event | category | flops | bytes accessed | tf_op | source)
XLA Modules:
  0.0 742.3 jit_solution(3466303294791412901)
XLA Ops:
  10.4 6.1 collective-permute-start
  58.8 8.5 %fusion.91 = f32[384,8,1536]{2,0,1:T(8,128)} fusion(bf16[384,8,384]{0,2,1:T(8,128)(2,1)S(1)} %bitcast.180, bf16[1536,192]{1,0:T(8,128)(2,1)S(1)} %copy-done.15), kind=kOutput, calls=%fused_computation.149 | convolution fusion | flops 3623878656 | bytes 21823488 | tf_op jit(solution)/shard_map/tmw,zw->tmz/dot_general | solution.py:46
  67.3 11.5 %fusion.87 = f32[384,10,1536]{2,0,1:T(8,128)} fusion(bf16[384,8,384]{0,2,1:T(8,128)(2,1)S(1)} %bitcast.181, bf16[1536,192]{1,0:T(8,128)(2,1)S(1)} %copy-done.11, bf16[1536,192]{1,0:T(8,128)(2,1)S(1)} %copy-done.13), kind=kOutput, calls=%fused_computation.145 | convolution fusion | flops 3626237952 | bytes 27131904 | tf_op jit(solution)/shard_map/jit(_pad)/pad | solution.py:64
  78.8 29.1 %fusion.182 = (bf16[384,10,1536]{2,0,1:T(8,128)(2,1)}, f32[384,10,1536]{2,0,1:T(8,128)}) fusion(bf16[384,8,384]{0,2,1:T(8,128)(2,1)} %bitcast.182, bf16[1536,192]{1,0:T(8,128)(2,1)S(1)} %copy.120, f32[384,10,1536]{2,0,1:T(8,128)} %fusion.87, f32[384,8,1536]{2,0,1:T(8,128)} %fusion.91), kind=kOutput, calls=%fused_computation.262 | convolution fusion | flops 3641573376 | bytes 80805888 | tf_op jit(solution)/shard_map/jit(_pad)/pad | solution.py:64
  145.4 9.2 %fusion.107 = f32[384,8,1536]{2,0,1:T(8,128)} fusion(bf16[384,9,384]{0,2,1:T(8,128)(2,1)S(1)} %bitcast.189, bf16[192,1536]{1,0:T(8,128)(2,1)S(1)} %copy-done.32, bf16[192,1536]{1,0:T(8,128)(2,1)S(1)} %copy-done.34), kind=kOutput, calls=%fused_computation.170 | convolution fusion | flops 3626237952 | bytes 22708224 | tf_op jit(solution)/shard_map/slice | solution.py:217
  154.6 21.0 %multiply_convert_fusion.1 = (bf16[384,8,1536]{2,0,1:T(8,128)(2,1)}, f32[384,8,1536]{2,0,1:T(8,128)}) fusion(f32[384,8,1536]{2,0,1:T(8,128)} %fusion.107, bf16[384,9,384]{0,2,1:T(8,128)(2,1)} %bitcast.190, bf16[192,1536]{1,0:T(8,128)(2,1)S(1)} %copy-done.48, bf16[192,1536]{1,0:T(8,128)(2,1)S(1)} %squeeze.28), kind=kOutput, calls=%fused_computation.36 | convolution fusion | flops 3673423872 | bytes 51019776 | tf_op jit(solution)/shard_map/slice | solution.py:217
  175.6 6.6 fusion.82
  188.6 5.8 collective-permute-start.4
  194.4 13.0 %slice.276 = f32[384,8,1536]{2,0,1:T(8,128)} slice(f32[384,10,1536]{2,0,1:T(8,128)} %get-tuple-element.109), slice={[0:384], [1:9], [0:1536]} | slice | bytes 37748736 | tf_op jit(solution)/shard_map/slice | solution.py:272
  207.6 25.9 %all-reduce.18.cloned.1.call-done = bf16[384,512]{1,0:T(8,128)(2,1)} async-done(((bf16[384,512]{1,0:T(8,128)(2,1)}), bf16[384,512]{1,0:T(8,128)(2,1)}) %all-reduce.18.cloned.1.call-update) | async-done | bytes 393232 | tf_op jit(solution)/shard_map/psum | solution.py:225
  256.4 7.9 %tile.28 = f32[384,8,32,48]{0,3,2,1:T(8,128)} broadcast(f32[384,8,48]{0,2,1:T(8,128)S(1)} %bitcast.200), dimensions={0,1,3} | broadcast | bytes 19464192 | tf_op jit(solution)/shard_map/tile | solution.py:233
  264.3 18.7 %copy.112 = f32[384,8,1536]{2,0,1:T(8,128)} copy(f32[384,8,1536]{0,2,1:T(8,128)} %bitcast.178) | data formatting | bytes 37748736 | tf_op jit(solution)/shard_map/tile | solution.py:233
  299.1 23.4 %fusion.25 = (f32[384,1536]{1,0:T(8,128)}, bf16[384,8,1536]{2,0,1:T(8,128)(2,1)}) fusion(bf16[384,8,1536]{2,0,1:T(8,128)(2,1)} %get-tuple-element.106, f32[384,8,1536]{2,0,1:T(8,128)} %fusion.72, f32[384,8,1536]{2,0,1:T(8,128)S(1)} %copy-done.2, f32[384,1536]{1,0:T(8,128)} %copy.111), kind=kLoop, calls=%fused_computation.33 | loop fusion | flops 117374976 | bytes 61341696
  327.7 6.6 convolution_convert_fusion.12
  341.5 39.1 %all-reduce.20.cloned.1.call-done = bf16[384,512]{1,0:T(8,128)(2,1)} async-done(((bf16[384,512]{1,0:T(8,128)(2,1)}), bf16[384,512]{1,0:T(8,128)(2,1)}) %all-reduce.20.cloned.1.call-update) | async-done | bytes 393232 | tf_op jit(solution)/shard_map/psum | solution.py:288
  419.8 7.0 concatenate.60
  429.1 7.8 %tile.31 = f32[384,8,32,48]{0,3,2,1:T(8,128)} broadcast(f32[384,8,48]{0,2,1:T(8,128)S(1)} %bitcast.199), dimensions={0,1,3} | broadcast | bytes 19464192 | tf_op jit(solution)/shard_map/tile | solution.py:300
  436.9 18.7 %copy.138 = f32[384,8,1536]{2,0,1:T(8,128)} copy(f32[384,8,1536]{0,2,1:T(8,128)} %bitcast.179) | data formatting | bytes 37748736 | tf_op jit(solution)/shard_map/tile | solution.py:300
  455.6 29.3 %fusion.12 = (bf16[384,8,1536]{2,0,1:T(8,128)(2,1)S(1)}, bf16[384,8,1536]{2,0,1:T(8,128)(2,1)S(1)}) fusion(f32[384,8,1536]{2,0,1:T(8,128)} %get-tuple-element.107, f32[384,8,1536]{2,0,1:T(8,128)} %copy.138, bf16[384,8,1536]{2,0,1:T(8,128)(2,1)} %get-tuple-element.80, f32[384,1536]{1,0:T(8,128)} %copy.111, f32[384,8,1536]{2,0,1:T(8,128)} %copy.112, ...), kind=kLoop, calls=%fused_computation.19 | loop fusion | flops 155713536 | bytes 96731136 | tf_op jit(solution)/shard_map/convert_element_type | solution.py:303
  485.0 8.1 %fusion.108 = f32[384,8,384]{0,2,1:T(8,128)} fusion(bf16[384,8,1536]{2,0,1:T(8,128)(2,1)S(1)} %get-tuple-element.99, bf16[192,1536]{1,0:T(8,128)(2,1)S(1)} %copy-done.49, bf16[192,1536]{1,0:T(8,128)(2,1)S(1)} %copy-done.51), kind=kOutput, calls=%fused_computation.171 | convolution fusion | flops 3626237952 | bytes 15335424 | tf_op jit(solution)/shard_map/tmz,wz->tmw/dot_general | solution.py:46
  512.1 8.9 %pad_add_fusion = f32[384,9,384]{0,2,1:T(8,128)S(1)} fusion(f32[384,8,384]{0,2,1:T(8,128)} %fusion.108, bf16[384,8,1536]{2,0,1:T(8,128)(2,1)S(1)} %get-tuple-element.99, bf16[192,1536]{1,0:T(8,128)(2,1)S(1)} %copy-done.33, bf16[192,1536]{1,0:T(8,128)(2,1)S(1)} %copy-done.35), kind=kOutput, calls=%fused_computation.66 | convolution fusion | flops 3627565056 | bytes 20643840 | tf_op jit(solution)/shard_map/jit(_pad)/pad | solution.py:64
  531.0 6.0 concatenate.68
  537.0 6.5 copy.140
  543.5 6.0 concatenate.67
  549.5 6.5 copy.139
  556.0 15.4 %all-reduce.11 = (bf16[512]{0:T(512)(128)(2,1)S(1)}, bf16[512]{0:T(512)(128)(2,1)S(1)}) all-reduce(bf16[512]{0:T(512)(128)(2,1)S(1)} %get-tuple-element.64, bf16[512]{0:T(512)(128)(2,1)S(1)} %get-tuple-element.62), channel_id=1, replica_groups=mesh['rows'=4,'frames'=8] {'frames'}, use_global_device_ids=true, to_apply=%region_17.18 | all-reduce | flops 1024 | bytes 4096 | tf_op jit(solution)/shard_map/psum | solution.py:340
  572.6 9.9 %fusion.98 = f32[4,4,3,48]{3,1,2,0:T(4,128)S(1)} fusion(f32[2,64,3,32,48]{1,4,3,2,0:T(8,128)} %copy.140, f32[2,64,3,32,48]{1,4,3,2,0:T(8,128)} %copy.139, s32[4,32]{0,1:T(8,128)S(1)} %copy-done.55), kind=kOutput, calls=%fused_computation.155 | convolution fusion | flops 57810944 | bytes 4728320 | tf_op jit(solution)/shard_map/kwj,hwcjo->hkco/dot_general | solution.py:310
  585.9 23.5 %fusion.53 = f32[1536,1152]{0,1:T(8,128)} fusion(bf16[384,8,384]{0,2,1:T(8,128)(2,1)} %bitcast.183, bf16[384,1,1536]{2,0,1:T(8,128)(2,1)} %collective-permute-done.3, bf16[384,8,1536]{2,0,1:T(8,128)(2,1)} %copy-done.5, bf16[384,1,1536]{2,0,1:T(8,128)(2,1)} %collective-permute-done.2), kind=kOutput, calls=%fused_computation.65 | convolution fusion | flops 13663272960 | bytes 21233664 | tf_op jit(solution)/shard_map/tmz,tmw->zw/dot_general | solution.py:46
  640.5 9.6 %fusion.95 = f32[4,4,48,3]{2,1,3,0:T(4,128)S(1)} fusion(f32[1,32,48,64,3]{3,2,1,4,0:T(8,128)} %copy.144, f32[1,32,48,64,3]{3,2,1,4,0:T(8,128)} %copy.143, f32[1,32,48,64,3]{3,2,1,4,0:T(8,128)} %copy.142, f32[1,32,48,64,3]{3,2,1,4,0:T(8,128)} %copy.141, s32[4,32]{0,1:T(8,128)S(1)} %copy-done.55), kind=kOutput, calls=%fused_computation.154 | convolution fusion | flops 60170240 | bytes 4728320 | tf_op jit(solution)/shard_map/kwj,hjowc->hkoc/dot_general | solution.py:258
  650.1 19.5 %fusion.56 = f32[384,10,1152]{2,0,1:T(8,128)} fusion(bf16[384,1,1536]{2,0,1:T(8,128)(2,1)} %collective-permute-done.3, bf16[384,8,1536]{2,0,1:T(8,128)(2,1)S(1)} %bitcast.188, bf16[384,1,1536]{2,0,1:T(8,128)(2,1)} %collective-permute-done.2, bf16[1536,1152]{1,0:T(8,128)(2,1)S(1)} %copy-done.21), kind=kOutput, calls=%fused_computation.67 | convolution fusion | flops 13601341440 | bytes 33030144 | tf_op jit(solution)/shard_map/tmz,zw->tmw/dot_general | solution.py:46
  669.6 7.4 fusion.57
  681.4 38.1 %all-reduce.10 = (f32[4,4,3,48]{3,1,2,0:T(4,128)}, f32[4,4,48,3]{2,1,3,0:T(4,128)}) all-reduce(f32[4,4,3,48]{3,1,2,0:T(4,128)S(1)} %fusion.98, f32[4,4,48,3]{2,1,3,0:T(4,128)S(1)} %fusion.95), channel_id=1, replica_groups=mesh['rows'=4,'frames'=8] {'rows','frames'}, use_global_device_ids=true, to_apply=%region_14.15 | all-reduce | flops 4608 | bytes 36864 | tf_op jit(solution)/shard_map/psum | solution.py:348
  (297 shorter events, 266.8 us)
Async XLA Ops:
  7.2 244.8 %copy-start = (bf16[512,2048]{1,0:T(8,128)(2,1)S(1)}, bf16[512,2048]{1,0:T(8,128)(2,1)}, u32[]{:S(2)}) copy-start(bf16[512,2048]{1,0:T(8,128)(2,1)} %param.32) | copy-start | bytes 6291460
  7.2 14.6 %copy-start.59 = (bf16[4,4,48,3]{2,1,3,0:T(4,128)(2,1)S(1)}, bf16[4,4,48,3]{2,1,3,0:T(4,128)(2,1)}, u32[]{:S(2)}) copy-start(bf16[4,4,48,3]{2,1,3,0:T(4,128)(2,1)} %param.37) | copy-start | bytes 13828
  7.2 226.3 %all-reduce.18.cloned.1.call-start = ((), (), s32[]{:S(2)}) async-start(), calls=%async_computation | async-start | bytes 786432 | tf_op jit(solution)/shard_map/psum | solution.py:225
  9.1 132.4 %collective-permute-start.1 = (bf16[384,1,192]{0,2,1:T(8,128)(2,1)}, bf16[384,1,192]{0,2,1:T(8,128)(2,1)}, u32[]{:S(2)}, u32[]{:S(2)}) collective-permute-start(bf16[384,1,192]{0,2,1:T(8,128)(2,1)} %get-tuple-element.102), channel_id=1, source_target_pairs={{8,0},{16,8},{24,16},{9,1},{17,9},{25,17},{10,2},{18,10},{26,18},{... | collective-permute-start | bytes 442376 | tf_op jit(solution)/shard_map/ppermute | solution.py:24
  10.4 131.1 %collective-permute-start = (bf16[384,1,192]{0,2,1:T(8,128)(2,1)}, bf16[384,1,192]{0,2,1:T(8,128)(2,1)}, u32[]{:S(2)}, u32[]{:S(2)}) collective-permute-start(bf16[384,1,192]{0,2,1:T(8,128)(2,1)} %get-tuple-element.101), channel_id=1, source_target_pairs={{0,8},{8,16},{16,24},{1,9},{9,17},{17,25},{2,10},{10,18},{18,26},{... | collective-permute-start | bytes 442376 | tf_op jit(solution)/shard_map/ppermute | solution.py:22
  32.1 46.7 %copy-start.9 = (bf16[1536,192]{1,0:T(8,128)(2,1)}, bf16[1536,192]{1,0:T(8,128)(2,1)S(1)}, u32[]{:S(2)}) copy-start(bf16[1536,192]{1,0:T(8,128)(2,1)S(1)} %copy.120) | copy-start | bytes 1769476
  56.7 10.6 %copy-start.61 = (pred[384]{0:T(512)(128)(4,1)}, pred[384]{0:T(512)(128)(4,1)S(1)}, u32[]{:S(2)}) copy-start(pred[384]{0:T(512)(128)(4,1)S(1)} %compare_and_fusion) | copy-start | bytes 1156
  58.7 8.6 %copy-start.3 = (bf16[384,16,192]{0,2,1:T(8,128)(2,1)}, bf16[384,16,192]{0,2,1:T(8,128)(2,1)S(1)}, u32[]{:S(2)}) copy-start(bf16[384,16,192]{0,2,1:T(8,128)(2,1)S(1)} %broadcast_select_fusion) | copy-start | bytes 7077892
  58.7 8.6 %copy-start.11 = (bf16[1536,192]{1,0:T(8,128)(2,1)S(1)}, bf16[1536,192]{1,0:T(8,128)(2,1)}, u32[]{:S(2)}) copy-start(bf16[1536,192]{1,0:T(8,128)(2,1)} %copy.119) | copy-start | bytes 1769476
  141.4 13.2 %copy-start.50 = (bf16[192,1536]{1,0:T(8,128)(2,1)}, bf16[192,1536]{1,0:T(8,128)(2,1)S(1)}, u32[]{:S(2)}) copy-start(bf16[192,1536]{1,0:T(8,128)(2,1)S(1)} %squeeze.28) | copy-start | bytes 1769476
  145.4 9.2 %copy-start.48 = (bf16[192,1536]{1,0:T(8,128)(2,1)S(1)}, bf16[192,1536]{1,0:T(8,128)(2,1)}, u32[]{:S(2)}) copy-start(bf16[192,1536]{1,0:T(8,128)(2,1)} %squeeze.29) | copy-start | bytes 1769476
  184.1 196.5 %all-reduce.20.cloned.1.call-start = ((), (), s32[]{:S(2)}) async-start(), calls=%async_computation.1 | async-start | bytes 786432 | tf_op jit(solution)/shard_map/psum | solution.py:288
  187.3 101.5 %collective-permute-start.5 = (bf16[384,1,1536]{2,0,1:T(8,128)(2,1)}, bf16[384,1,1536]{2,0,1:T(8,128)(2,1)}, u32[]{:S(2)}, u32[]{:S(2)}) collective-permute-start(bf16[384,1,1536]{2,0,1:T(8,128)(2,1)} %get-tuple-element.82), channel_id=1, source_target_pairs={{8,0},{16,8},{24,16},{9,1},{17,9},{25,17},{10,2},{18,10},{26,18},{... | collective-permute-start | bytes 3538952 | tf_op jit(solution)/shard_map/ppermute | solution.py:24
  188.6 100.3 %collective-permute-start.4 = (bf16[384,1,1536]{2,0,1:T(8,128)(2,1)}, bf16[384,1,1536]{2,0,1:T(8,128)(2,1)}, u32[]{:S(2)}, u32[]{:S(2)}) collective-permute-start(bf16[384,1,1536]{2,0,1:T(8,128)(2,1)} %get-tuple-element.81), channel_id=1, source_target_pairs={{0,8},{8,16},{16,24},{1,9},{9,17},{17,25},{2,10},{10,18},{18,26},{... | collective-permute-start | bytes 3538952 | tf_op jit(solution)/shard_map/ppermute | solution.py:22
  194.4 41.4 %copy-start.60 = (f32[512]{0:T(512)S(1)}, f32[512]{0:T(512)}, u32[]{:S(2)}) copy-start(f32[512]{0:T(512)} %param.28) | copy-start | bytes 6148
  264.3 18.7 %copy-start.56 = (bf16[512,48]{0,1:T(8,128)(2,1)S(1)}, bf16[512,48]{0,1:T(8,128)(2,1)}, u32[]{:S(2)}) copy-start(bf16[512,48]{0,1:T(8,128)(2,1)} %param.35) | copy-start | bytes 147460
  288.9 10.2 %copy-start.2 = (f32[384,8,1536]{2,0,1:T(8,128)S(1)}, f32[384,8,1536]{2,0,1:T(8,128)}, u32[]{:S(2)}) copy-start(f32[384,8,1536]{2,0,1:T(8,128)} %copy.112) | copy-start | bytes 56623108
  327.6 8.6 %copy-start.62 = (pred[384]{0:T(512)(128)(4,1)S(1)}, pred[384]{0:T(512)(128)(4,1)}, u32[]{:S(2)}) copy-start(pred[384]{0:T(512)(128)(4,1)} %copy-done.61) | copy-start | bytes 1156
  336.1 383.4 %all-reduce.24.cloned.1.call-start = ((), (), s32[]{:S(2)}) async-start(), calls=%async_computation.3 | async-start | bytes 16252928 | tf_op jit(solution)/shard_map/psum | solution.py:338
  417.9 316.1 %all-reduce.22.cloned.1.call-start = ((), (), s32[]{:S(2)}) async-start(), calls=%async_computation.2 | async-start | bytes 196608 | tf_op jit(solution)/shard_map/psum | solution.py:348
  455.6 29.3 %copy-start.49 = (bf16[192,1536]{1,0:T(8,128)(2,1)S(1)}, bf16[192,1536]{1,0:T(8,128)(2,1)}, u32[]{:S(2)}) copy-start(bf16[192,1536]{1,0:T(8,128)(2,1)} %squeeze.29) | copy-start | bytes 1769476
  455.6 29.3 %copy-start.51 = (bf16[192,1536]{1,0:T(8,128)(2,1)S(1)}, bf16[192,1536]{1,0:T(8,128)(2,1)}, u32[]{:S(2)}) copy-start(bf16[192,1536]{1,0:T(8,128)(2,1)} %copy-done.50) | copy-start | bytes 1769476
  484.9 18.7 %copy-start.5 = (bf16[384,8,1536]{2,0,1:T(8,128)(2,1)}, bf16[384,8,1536]{2,0,1:T(8,128)(2,1)S(1)}, u32[]{:S(2)}) copy-start(bf16[384,8,1536]{2,0,1:T(8,128)(2,1)S(1)} %get-tuple-element.100) | copy-start | bytes 28311556
  505.2 80.7 %collective-permute-start.3 = (bf16[384,1,1536]{2,0,1:T(8,128)(2,1)}, bf16[384,1,1536]{2,0,1:T(8,128)(2,1)}, u32[]{:S(2)}, u32[]{:S(2)}) collective-permute-start(bf16[384,1,1536]{2,0,1:T(8,128)(2,1)} %get-tuple-element.84), channel_id=1, source_target_pairs={{8,0},{16,8},{24,16},{9,1},{17,9},{25,17},{10,2},{18,10},{26,18},{... | collective-permute-start | bytes 3538952 | tf_op jit(solution)/shard_map/ppermute | solution.py:24
  506.5 79.4 %collective-permute-start.2 = (bf16[384,1,1536]{2,0,1:T(8,128)(2,1)}, bf16[384,1,1536]{2,0,1:T(8,128)(2,1)}, u32[]{:S(2)}, u32[]{:S(2)}) collective-permute-start(bf16[384,1,1536]{2,0,1:T(8,128)(2,1)} %get-tuple-element.83), channel_id=1, source_target_pairs={{0,8},{8,16},{16,24},{1,9},{9,17},{17,25},{2,10},{10,18},{18,26},{... | collective-permute-start | bytes 3538952 | tf_op jit(solution)/shard_map/ppermute | solution.py:22
  525.2 57.3 %collective-permute-start.7 = (bf16[384,1,192]{0,2,1:T(8,128)(2,1)S(1)}, bf16[384,1,192]{0,2,1:T(8,128)(2,1)S(1)}, u32[]{:S(2)}, u32[]{:S(2)}) collective-permute-start(bf16[384,1,192]{0,2,1:T(8,128)(2,1)S(1)} %get-tuple-element.98), channel_id=1, source_target_pairs={{8,0},{16,8},{24,16},{9,1},{17,9},{25,17},{10,2},{18,10},{26,18},{... | collective-permute-start | bytes 442376 | tf_op jit(solution)/shard_map/ppermute | solution.py:24
  526.5 56.1 %collective-permute-start.6 = (bf16[384,1,192]{0,2,1:T(8,128)(2,1)S(1)}, bf16[384,1,192]{0,2,1:T(8,128)(2,1)S(1)}, u32[]{:S(2)}, u32[]{:S(2)}) collective-permute-start(bf16[384,1,192]{0,2,1:T(8,128)(2,1)S(1)} %get-tuple-element.97), channel_id=1, source_target_pairs={{0,8},{8,16},{16,24},{1,9},{9,17},{17,25},{2,10},{10,18},{18,26},{... | collective-permute-start | bytes 442376 | tf_op jit(solution)/shard_map/ppermute | solution.py:22
  549.5 23.1 %copy-start.55 = (s32[4,32]{0,1:T(8,128)S(1)}, s32[4,32]{0,1:T(8,128)}, u32[]{:S(2)}) copy-start(s32[4,32]{0,1:T(8,128)} %copy-done.54) | copy-start | bytes 1540
  636.8 13.3 %slice-start = ((s8[9437184]{0:T(1024)(128)(4,1)}), s8[1048576]{0:T(1024)(128)(4,1)S(1)}, s32[]{:S(2)}) async-start(s8[9437184]{0:T(1024)(128)(4,1)} %bitcast.187), calls=%async_computation.4 | async-start | bytes 2097152
  640.5 9.6 %slice-start.1 = ((s8[9437184]{0:T(1024)(128)(4,1)}), s8[4194304]{0:T(1024)(128)(4,1)S(1)}, s32[]{:S(2)}) async-start(s8[9437184]{0:T(1024)(128)(4,1)} %bitcast.187), calls=%async_computation.5 | async-start | bytes 8388608
  640.5 9.6 %slice-start.2 = ((s8[9437184]{0:T(1024)(128)(4,1)}), s8[4194304]{0:T(1024)(128)(4,1)S(1)}, s32[]{:S(2)}) async-start(s8[9437184]{0:T(1024)(128)(4,1)} %bitcast.187), calls=%async_computation.6 | async-start | bytes 8388608
  640.5 9.7 %copy-start.21 = (bf16[1536,1152]{1,0:T(8,128)(2,1)S(1)}, bf16[1536,1152]{1,0:T(8,128)(2,1)}, u32[]{:S(2)}) copy-start(bf16[1536,1152]{1,0:T(8,128)(2,1)} %concatenate.60) | copy-start | bytes 10616836
  (50 other events, 181.1 us)
Sparse Core Ops, SparseCore 0:
  184.2 49.2 all-reduce.17
  336.3 44.2 all-reduce.19
  418.1 173.1 all-reduce.23
  597.2 120.6 all-reduce.21
where the time goes:
time: 750 us; the launch traced here: 742 us
  local copies, waits for them, and re-layouts  243 us (32%)
  matrix products  240 us (32%)
  other arithmetic  99.2 us (13%)
  waiting for transfers between devices  65.1 us (9%)
  blocking collectives  53.5 us (7%)
  starting transfers between devices  27.4 us (4%)
  between operations  14.9 us (2%)
    dot_general x36, matrix products, product(): jnp.einsum(pattern, lhs_array, rhs_array, preferred_element_type=jnp.floa...  131 us
    pad x3, matrix products, pad_rows(): return jnp.pad(values, ((0, 0), (before, after), (0, 0)))  49.4 us
    psum x1, waiting for transfers between devices, on_device(): lax.psum(grad_film.astype(jnp.bfloat16), 'rows').astype(jnp.float32)  39.1 us
    psum x1, blocking collectives, on_device(): lax.psum((enc_kernel_grad, dec_kernel_grad, film_scale_grad), ('rows', 'f...  38.1 us
    slice x2, matrix products, on_device(): encoded = front_all[:, :-1] + back_all[:, 1:]  30.2 us
    convert_element_type x1, other arithmetic, on_device(): grad_encoded = (grad_features * gelu_slope(encoded)).astype(jnp.bfloat16)  29.3 us
    another operation x8, local copies, waits for them, and re-layouts, on_device(): jnp.stack([dec_cov[:, 2 * pair_width + line_width:], dec_cov[:, pair_widt...  26.8 us
    another operation x2, local copies, waits for them, and re-layouts, on_device(): jnp.tile(shift_rows.reshape(frame_count, map_rows, channels), (1, 1, map_...  26.6 us
  transfers between devices with their start and end apart: 12, of which 2 were waited for; matrix products, arithmetic and copies ran while one was open for 60% of the time, Pallas kernels for 0%

commit v1 on v0

v1 whole, which is shorter than its diff:
```python
import functools
import math

import jax
import jax.numpy as jnp
import numpy as np
from jax import lax
from jax.experimental import pallas as pl
from jax.experimental.pallas import tpu as pltpu
from jax.sharding import PartitionSpec as P

HEADS = 8
BF = jnp.bfloat16
F32 = jnp.float32
GROUPS = 4
SLOT = 64
PAD = 8
TILE = 384
ROOT = math.sqrt(2.0 / math.pi)
CUBE = 0.044715
MIB = 1024 * 1024


def nn(lhs, rhs):
    return lax.dot_general(lhs, rhs, (((1,), (0,)), ((), ())), preferred_element_type=F32)


def nt(lhs, rhs):
    return lax.dot_general(lhs, rhs, (((1,), (1,)), ((), ())), preferred_element_type=F32)


def tn(lhs, rhs):
    return lax.dot_general(lhs, rhs, (((0,), (0,)), ((), ())), preferred_element_type=F32)


def tt(lhs, rhs):
    return lax.dot_general(lhs, rhs, (((0,), (1,)), ((), ())), preferred_element_type=F32)


SHRINK = (ROOT * CUBE) ** (1.0 / 3.0)
BEND = ROOT / SHRINK


def gelu_of_half(half):
    bend = half * ((8.0 * ROOT * CUBE) * (half * half) + 2.0 * ROOT)
    return half * (jnp.tanh(bend.astype(F32)) + 1.0).astype(BF)


def double_slope(shrunk):
    square = shrunk * shrunk
    bend = shrunk * (square + BEND)
    level = jnp.tanh(bend.astype(F32))
    rise, fall = (1.0 + level).astype(BF), (1.0 - level).astype(BF)
    return rise * (shrunk * (3.0 * square + BEND) * fall + 1.0)


def gelu_pair(value):
    square = value * value
    bend = (ROOT * CUBE) * square + ROOT
    gate = 0.5 * jnp.tanh(value * bend) + 0.5
    result = value * gate
    slope = gate + result * (1.0 - gate) * ((6.0 * ROOT * CUBE) * square + 2.0 * ROOT)
    return result, slope


def wide_sum(parts):
    total = None
    for k in range(0, len(parts), 4):
        some = parts[k : k + 4]
        while len(some) > 1:
            some = [a + b for a, b in zip(some[::2], some[1::2])]
        total = some[0].astype(F32) if total is None else total + some[0].astype(F32)
    return total


def whole(shape):
    return pl.BlockSpec(shape, lambda *_: (0,) * len(shape))


def params(mib):
    return pltpu.CompilerParams(vmem_limit_bytes=mib * MIB)


def cost(flops, nbytes, transcendentals=0):
    return pl.CostEstimate(flops=flops, bytes_accessed=nbytes, transcendentals=transcendentals)


def tap_places(taps, chan_in, copies):
    places = np.zeros((copies, taps * chan_in * taps, taps * SLOT), np.float32)
    for j in range(copies):
        for kh in range(taps):
            for c in range(chan_in):
                for kw in range(taps):
                    place = PAD - chan_in + (2 * j + kw) * chan_in + c
                    places[j, (kh * chan_in + c) * taps + kw, kh * SLOT + place] = 1.0
    return places


def expand_kernel(enc_ref, dec_ref, places_ref, enc_cols_out, enc_out, dec_cols_out, dec_out):
    for source, cols, out in ((enc_ref, enc_cols_out, enc_out), (dec_ref, dec_cols_out, dec_out)):
        taps = source[...]
        spread = jnp.concatenate([tn(taps, places_ref[j]) for j in range(places_ref.shape[0])], axis=0)
        cols[...] = spread.astype(BF)
        out[...] = jnp.transpose(spread).astype(BF)


def expand(enc_taps, dec_taps, places):
    copies, channels, size = places.shape
    width = copies * enc_taps.shape[1]
    cols = jax.ShapeDtypeStruct((width, size), BF)
    rows = jax.ShapeDtypeStruct((size, width), BF)
    return pl.pallas_call(
        expand_kernel,
        out_shape=[cols, rows, cols, rows],
        compiler_params=params(60),
        name="expand",
    )(enc_taps, dec_taps, places)


def keep_row(ring_ref, slot, row):
    ring_ref[slot, PAD : PAD + row.shape[0], :] = row


def window(ring_ref, first, taps, g, stride):
    return jnp.concatenate(
        [ring_ref[lax.rem(first + kh, 4), g * stride : g * stride + SLOT, :] for kh in range(taps)], axis=0
    )


def fold_taps(cov_ref, places_ref, channels):
    total = None
    for j in range(places_ref.shape[0]):
        term = lax.dot_general(
            places_ref[j].astype(F32),
            cov_ref[j * channels : (j + 1) * channels, :],
            (((1,), (1,)), ((), ())),
            precision=lax.Precision.HIGHEST,
            preferred_element_type=F32,
        )
        total = term if total is None else total + term
    return total


def halo_spec(halo, which):
    return pl.BlockSpec((1,) + halo.shape[1:], lambda i: (which, 0, 0))


def four_row_specs(frames, lanes, rows, base=0):
    return [
        pl.BlockSpec((1, lanes, frames), lambda i, k=k: (jnp.minimum(4 * (i + base) + k, rows - 1), 0, 0))
        for k in range(1, 5)
    ]


def fill_six(ring_scr, first, last, start, row_refs, down_ref, live=None):
    def masked(row):
        return row if live is None else (row.astype(F32) * live).astype(BF)

    @pl.when(first)
    def _():
        ring_scr[...] = jnp.zeros_like(ring_scr)
        for slot, row in enumerate(start):
            keep_row(ring_scr, slot, masked(row()))

    @pl.when(jnp.logical_not(first))
    def _():
        ring_scr[0:2] = ring_scr[4:6]

    for k, ref in enumerate(row_refs[:3]):
        keep_row(ring_scr, k + 2, masked(ref[0]))

    @pl.when(jnp.logical_not(last))
    def _():
        keep_row(ring_scr, 5, masked(row_refs[3][0]))

    @pl.when(last)
    def _():
        keep_row(ring_scr, 5, masked(down_ref[0]))


def fill_windows_at(window_scr, ring_scr, first, taps, stride):
    frames = ring_scr.shape[2]
    for g in range(GROUPS):
        for kh in range(taps):
            window_scr[kh * SLOT : (kh + 1) * SLOT, g * frames : (g + 1) * frames] = ring_scr[
                first + kh, g * stride : g * stride + SLOT, :
            ]


def add_rows(rows_scr, first, placed, g, stride):
    for kh in range(placed.shape[0] // SLOT):
        part = slice(g * stride, g * stride + SLOT)
        rows_scr[first + kh, part, :] += placed[kh * SLOT : (kh + 1) * SLOT, :]


def fill_windows(window_scr, ring_scr, first, taps, stride):
    frames = ring_scr.shape[2]
    for g in range(GROUPS):
        window_scr[:, g * frames : (g + 1) * frames] = window(ring_scr, first, taps, g, stride)


def tiles(frames, g):
    size = min(TILE, frames)
    return [(slice(t, t + size), slice(g * frames + t, g * frames + t + size)) for t in range(0, frames, size)]


def encode_row(ring_scr, first, enc_ref, feat_out, window_scr, value_scr, sum_scr, stride):
    width, depth = enc_ref.shape
    channels, frames = sum_scr.shape
    fill_windows(window_scr, ring_scr, first, depth // SLOT, stride)
    value_scr[...] = nn(enc_ref[...] * 0.5, window_scr[...])
    for g in range(GROUPS):
        for tile, column in tiles(frames, g):
            found = []
            for j in range(0, width, channels):
                low = gelu_of_half(value_scr[j : j + channels, column].astype(BF))
                feat_out[0, g * width + j : g * width + j + channels, tile] = low
                found.append(low)
            sum_scr[:, tile] = wide_sum(found) if g == 0 else sum_scr[:, tile] + wide_sum(found)
    return (sum_scr[...] * (1.0 / (GROUPS * width // channels))).astype(BF)


def encode_inner_kernel(
    odd_ref, even_ref, one_ref, two_ref, enc_ref, feat_out, profile_out, ring_scr, window_scr, value_scr, sum_scr
):
    step = pl.program_id(0)

    @pl.when(step == 0)
    def _():
        ring_scr[...] = jnp.zeros_like(ring_scr)
        keep_row(ring_scr, 2, one_ref[0])
        keep_row(ring_scr, 3, two_ref[0])

    keep_row(ring_scr, lax.rem(2 * step, 4), odd_ref[0])
    keep_row(ring_scr, lax.rem(2 * step + 1, 4), even_ref[0])
    stride = odd_ref.shape[1] // GROUPS
    profile_out[...] = encode_row(
        ring_scr, 2 * step + 2, enc_ref, feat_out, window_scr, value_scr, sum_scr, stride
    )


def encode_edge_kernel(
    a_ref, b_ref, c_ref, up_ref, down_ref, enc_ref, emb_ref, inner_ref, feat_ref,
    feat_out, profile_out, embed_out, ring_scr, window_scr, value_scr, sum_scr,
):
    del feat_ref
    step = pl.program_id(0)
    channels = sum_scr.shape[0]

    @pl.when(step == 0)
    def _():
        ring_scr[...] = jnp.zeros_like(ring_scr)
        keep_row(ring_scr, 0, up_ref[0])
        for k, ref in enumerate((a_ref, b_ref, c_ref)):
            keep_row(ring_scr, k + 1, ref[0])

    @pl.when(step == 1)
    def _():
        for k, ref in enumerate((a_ref, b_ref, c_ref)):
            keep_row(ring_scr, k, ref[0])
        keep_row(ring_scr, 3, down_ref[0])

    stride = up_ref.shape[1] // GROUPS
    profile = encode_row(ring_scr, 0, enc_ref, feat_out, window_scr, value_scr, sum_scr, stride)
    size = profile_out.shape[0]

    @pl.when(step == 0)
    def _():
        profile_out[:channels, :] = profile
        profile_out[channels : size - channels, :] = inner_ref[...]

    @pl.when(step == 1)
    def _():
        profile_out[size - channels :, :] = profile
        embed_out[...] = tn(profile_out[...], emb_ref[...]).astype(BF)


def encode_inner(image_rows, enc, channels):
    rows, lanes, frames = image_rows.shape
    map_rows = rows // 2
    width = enc.shape[0]
    line = GROUPS * width
    map_spec = pl.BlockSpec((1, line, frames), lambda i: (i + 1, 0, 0))
    map_shape = jax.ShapeDtypeStruct((map_rows, line, frames), BF)
    inner = map_rows - 2
    return pl.pallas_call(
        encode_inner_kernel,
        grid=(inner,),
        in_specs=[
            pl.BlockSpec((1, lanes, frames), lambda i: (2 * i + 3, 0, 0)),
            pl.BlockSpec((1, lanes, frames), lambda i: (2 * i + 4, 0, 0)),
            pl.BlockSpec((1, lanes, frames), lambda i: (1, 0, 0)),
            pl.BlockSpec((1, lanes, frames), lambda i: (2, 0, 0)),
            whole(enc.shape),
        ],
        out_specs=[map_spec, pl.BlockSpec((channels, frames), lambda i: (i, 0))],
        out_shape=[map_shape, jax.ShapeDtypeStruct((inner * channels, frames), BF)],
        scratch_shapes=[
            pltpu.VMEM((4, lanes + 2 * PAD, frames), BF),
            pltpu.VMEM((enc.shape[1], GROUPS * frames), BF),
            pltpu.VMEM((width, GROUPS * frames), F32),
            pltpu.VMEM((channels, frames), F32),
        ],
        compiler_params=params(60),
        cost_estimate=cost(2 * inner * frames * line * 256, 4 * inner * frames * line, inner * frames * line),
        name="encode_inner",
    )(image_rows, image_rows, image_rows, image_rows, enc)


def encode_edge(image_rows, up, down, enc, emb, inner, feat):
    rows, lanes, frames = image_rows.shape
    map_rows, line, _ = feat.shape
    width = enc.shape[0]
    channels = emb.shape[0] // map_rows
    model = emb.shape[1]
    end = map_rows - 1
    map_spec = pl.BlockSpec((1, line, frames), lambda i: (i * end, 0, 0))
    map_shape = jax.ShapeDtypeStruct(feat.shape, BF)
    profile = (map_rows * channels, frames)
    row_specs_here = [
        pl.BlockSpec((1, lanes, frames), lambda i, k=k: (i * (rows - 3) + k, 0, 0)) for k in range(3)
    ]
    return pl.pallas_call(
        encode_edge_kernel,
        grid=(2,),
        in_specs=row_specs_here
        + [halo_spec(up, 0), halo_spec(down, 0)]
        + [whole(x.shape) for x in (enc, emb, inner)]
        + [pl.BlockSpec(memory_space=pl.ANY)],
        out_specs=[map_spec, whole(profile), whole((frames, model))],
        out_shape=[
            map_shape,
            jax.ShapeDtypeStruct(profile, BF),
            jax.ShapeDtypeStruct((frames, model), BF),
        ],
        scratch_shapes=[
            pltpu.VMEM((4, lanes + 2 * PAD, frames), BF),
            pltpu.VMEM((enc.shape[1], GROUPS * frames), BF),
            pltpu.VMEM((width, GROUPS * frames), F32),
            pltpu.VMEM((channels, frames), F32),
        ],
        input_output_aliases={8: 0},
        compiler_params=params(60),
        cost_estimate=cost(4 * frames * line * 256, 8 * frames * line, 2 * frames * line),
        name="encode_edge",
    )(image_rows, image_rows, image_rows, up, down, enc, emb, inner, feat)


def normed(values):
    center = values - jnp.mean(values, axis=-1, keepdims=True)
    spread = jnp.mean(center * center, axis=-1, keepdims=True)
    inverse = lax.rsqrt(spread + 1e-05)
    return center * inverse, inverse


def stacked_heads(pair, lane):
    zero = jnp.zeros_like(pair)
    first = lane < 64
    return jnp.concatenate([jnp.where(first, pair, zero), jnp.where(first, zero, pair)], axis=0)


def fetch(sources, targets, sems):
    copies = [pltpu.make_async_copy(src, dst, sems.at[k]) for k, (src, dst) in enumerate(zip(sources, targets))]
    for copy in copies:
        copy.start()
    return copies


def send(source, target, sem):
    copy = pltpu.make_async_copy(source, target, sem)
    copy.start()
    return copy


def block_forward_kernel(
    slots, part_ref, more_ref, keys_ok_ref, ln1_ref, ln2_ref, film_scale_ref, qkv_in, out_in, up_in, down_in,
    film_shift_in, joined_out, attend_out, context_out, middle_out, active_out, slope_out, state_out, scale_out,
    shift_out, qkv_ref, out_ref, up_ref, down_ref, film_shift_ref, joined_ref, attend_ref, context_ref, middle_ref,
    active_ref, slope_ref, in_sems, out_sems,
):
    copies = fetch(
        (qkv_in, out_in, up_in, down_in, film_shift_in), (qkv_ref, out_ref, up_ref, down_ref, film_shift_ref), in_sems
    )
    embedded = part_ref[...].astype(F32) + more_ref[...].astype(F32)
    frames, model = embedded.shape
    unit, _ = normed(embedded)
    low = (unit * ln1_ref[...]).astype(BF)
    copies[0].wait()
    joined_ref[...] = nn(low, qkv_ref[...]).astype(BF)
    sent = [send(joined_ref, joined_out, out_sems.at[0])]
    size = 128
    row = lax.broadcasted_iota(jnp.int32, (size, size), 0)
    col = lax.broadcasted_iota(jnp.int32, (size, size), 1)
    inside = (row // slots == col // slots) & (col <= row)
    scaling = 1.0 / math.sqrt(model // HEADS)
    for b in range(frames // size):
        part = slice(b * size, (b + 1) * size)
        allowed = inside & (keys_ok_ref[:, part] > 0.5)
        for pair in range(HEADS // 2):
            lanes = pair * 128
            queries = joined_ref[part, lanes : lanes + 128]
            keys = stacked_heads(joined_ref[part, model + lanes : model + lanes + 128], col)
            values = stacked_heads(joined_ref[part, 2 * model + lanes : 2 * model + lanes + 128], col)
            scores = nt(queries, keys) * scaling
            halves = []
            for half in range(2):
                some = jnp.where(allowed, scores[:, half * size : (half + 1) * size], -1e30)
                weights = jnp.exp(some - jnp.max(some, axis=-1, keepdims=True))
                weights = weights / jnp.sum(weights, axis=-1, keepdims=True)
                halves.append(weights.astype(BF))
            weights = jnp.concatenate(halves, axis=1)
            attend_ref[b * HEADS // 2 + pair] = weights
            context_ref[part, lanes : lanes + 128] = nn(weights, values).astype(BF)
    sent.append(send(attend_ref, attend_out, out_sems.at[1]))
    sent.append(send(context_ref, context_out, out_sems.at[2]))
    copies[1].wait()
    middle = embedded + nn(context_ref[...], out_ref[...])
    middle_ref[...] = middle
    sent.append(send(middle_ref, middle_out, out_sems.at[3]))
    unit, _ = normed(middle)
    low = (unit * ln2_ref[...]).astype(BF)
    hidden = up_ref.shape[1]
    copies[2].wait()
    for start in range(0, hidden, 512):
        lanes = slice(start, start + 512)
        result, slope = gelu_pair(nn(low, up_ref[:, lanes]))
        active_ref[:, lanes] = result.astype(BF)
        slope_ref[:, lanes] = slope.astype(BF)
    sent.append(send(active_ref, active_out, out_sems.at[4]))
    sent.append(send(slope_ref, slope_out, out_sems.at[5]))
    copies[3].wait()
    state = (middle + nn(active_ref[...], down_ref[...])).astype(BF)
    state_out[...] = state
    scale_out[...] = nt(film_scale_ref[...], state) + 1.0
    copies[4].wait()
    shift_out[...] = tt(film_shift_ref[...], state)
    for copy in sent:
        copy.wait()


def block_forward(slots, parts, keys_ok, ln1, qkv, out_w, ln2, up_w, down_w, film_scale, film_shift):
    frames, model = parts[0].shape
    hidden = up_w.shape[1]
    blocks = frames // 128
    saved = [
        ((frames, 3 * model), BF),
        ((blocks * HEADS // 2, 128, 256), BF),
        ((frames, model), BF),
        ((frames, model), F32),
        ((frames, hidden), BF),
        ((frames, hidden), BF),
    ]
    shapes = [
        ((frames, model), BF),
        ((film_scale.shape[0], frames), F32),
        ((film_shift.shape[1], frames), F32),
    ]
    flops = 2 * frames * model * (3 * model + model + 2 * hidden)
    vmem, hbm = pl.BlockSpec(memory_space=pltpu.VMEM), pl.BlockSpec(memory_space=pl.ANY)
    staged = (qkv, out_w, up_w, down_w, film_shift)
    return pl.pallas_call(
        functools.partial(block_forward_kernel, slots),
        in_specs=[vmem] * 6 + [hbm] * len(staged),
        out_specs=[hbm] * len(saved) + [vmem] * len(shapes),
        out_shape=[jax.ShapeDtypeStruct(*s) for s in saved + shapes],
        scratch_shapes=[pltpu.VMEM(w.shape, w.dtype) for w in staged]
        + [pltpu.VMEM(*s) for s in saved]
        + [pltpu.SemaphoreType.DMA((len(staged),)), pltpu.SemaphoreType.DMA((len(saved),))],
        compiler_params=params(60),
        cost_estimate=cost(flops, 16 * 1024 * 1024, frames * hidden),
        name="block_forward",
    )(*parts, keys_ok, ln1, ln2, film_scale, *staged)


def decoded_grad_kernel(base, odd, a_ref, b_ref, c_ref, d_ref, one_ref, two_ref, down_ref, live_ref, dec_ref, *rest):
    out_ref, ring_scr, window_scr, grad_scr = rest[-4:]
    step = pl.program_id(0)
    _, lanes, frames = down_ref.shape
    width, depth = dec_ref.shape
    start = (lambda: one_ref[0], lambda: two_ref[0])
    fill_six(
        ring_scr, step == 0, step + base == odd, start, (a_ref, b_ref, c_ref, d_ref), down_ref, live_ref[...]
    )
    dec = dec_ref[...] * 0.5
    for r in range(2):
        fill_windows_at(window_scr, ring_scr, 2 * r, depth // SLOT, lanes // GROUPS)
        grad_scr[...] = nn(dec, window_scr[...])
        for g in range(GROUPS):
            for tile, column in tiles(frames, g):
                out_ref[r, g * width : (g + 1) * width, tile] = grad_scr[:, column].astype(BF)


def decoded_grad(recon_rows, up, down, live, dec_cols, base, steps, before):
    rows, lanes, frames = recon_rows.shape
    map_rows = rows // 2
    width, depth = dec_cols.shape
    line = GROUPS * width
    one = up if base == 0 else recon_rows
    row_shape = (1, lanes, frames)
    return pl.pallas_call(
        functools.partial(decoded_grad_kernel, base, map_rows // 2 - 1),
        grid=(steps,),
        in_specs=four_row_specs(frames, lanes, rows, base)
        + [
            halo_spec(up, 1) if base == 0 else pl.BlockSpec(row_shape, lambda i: (4 * base - 1, 0, 0)),
            pl.BlockSpec(row_shape, lambda i: (4 * base, 0, 0)),
            halo_spec(down, 1),
            whole(live.shape),
            whole(dec_cols.shape),
        ]
        + [pl.BlockSpec(memory_space=pl.ANY)] * len(before),
        out_specs=pl.BlockSpec((2, line, frames), lambda i: (i + base, 0, 0)),
        out_shape=jax.ShapeDtypeStruct((map_rows, line, frames), BF),
        scratch_shapes=[
            pltpu.VMEM((6, lanes + 2 * PAD, frames), BF),
            pltpu.VMEM((depth, GROUPS * frames), BF),
            pltpu.VMEM((width, GROUPS * frames), F32),
        ],
        input_output_aliases={9: 0} if before else {},
        compiler_params=params(60),
        cost_estimate=cost(4 * steps * frames * line * 256, 4 * steps * frames * line),
        name="decoded_grad",
    )(*[recon_rows] * 4, one, recon_rows, down, live, dec_cols, *before)


def decode_kernel(
    feat_ref, grad_ref, scale_ref, shift_ref, film_scale_ref, film_shift_ref,
    back_out, scale_grad_out, shift_grad_out, film_out, scale_scr, shift_grad_scr,
):
    step = pl.program_id(0)
    last = pl.num_programs(0) - 1
    channels, frames = scale_scr.shape
    line = feat_ref.shape[1]

    @pl.when(step == 0)
    def _():
        scale_scr[...] = jnp.zeros_like(scale_scr)

    scale = (scale_ref[...] * SHRINK).astype(BF)
    scaled = None
    for r in range(2):
        shift = (shift_ref[r * channels : (r + 1) * channels, :] * SHRINK).astype(BF)
        total = None
        for g in range(0, line, 4 * channels):
            backs, terms = [], []
            for j in range(g, g + 4 * channels, channels):
                rows = slice(j, j + channels)
                feat = feat_ref[r, rows, :]
                back = grad_ref[r, rows, :] * double_slope(feat * scale + shift)
                back_out[r, rows, :] = back
                backs.append(back)
                terms.append(back * feat)
            total = wide_sum(backs) if total is None else total + wide_sum(backs)
            scaled = wide_sum(terms) if scaled is None else scaled + wide_sum(terms)
        shift_grad_scr[2 * step + r] = total.astype(BF)
    scale_scr[...] += scaled

    @pl.when(step == last)
    def _():
        scale_grad = scale_scr[...].astype(BF)
        shift_grad = shift_grad_scr[...].reshape(shift_grad_out.shape)
        scale_grad_out[...] = scale_grad
        shift_grad_out[...] = shift_grad
        film_out[...] = (tn(scale_grad, film_scale_ref[...]) + tt(shift_grad, film_shift_ref[...])).astype(BF)


def decode(feat, grad, scale, shift, film_scale, film_shift):
    map_rows, line, frames = feat.shape
    channels, model = film_scale.shape
    map_spec = pl.BlockSpec((2, line, frames), lambda i: (i, 0, 0))
    grads = [
        jax.ShapeDtypeStruct((channels, frames), BF),
        jax.ShapeDtypeStruct((map_rows * channels, frames), BF),
        jax.ShapeDtypeStruct((frames, model), BF),
    ]
    return pl.pallas_call(
        decode_kernel,
        grid=(map_rows // 2,),
        in_specs=[
            map_spec,
            map_spec,
            whole(scale.shape),
            pl.BlockSpec((2 * channels, frames), lambda i: (i, 0)),
            whole(film_scale.shape),
            whole(film_shift.shape),
        ],
        out_specs=[map_spec] + [whole(g.shape) for g in grads],
        out_shape=[jax.ShapeDtypeStruct((map_rows, line, frames), BF)] + grads,
        scratch_shapes=[
            pltpu.VMEM((channels, frames), F32),
            pltpu.VMEM((map_rows, channels, frames), BF),
        ],
        compiler_params=params(60),
        cost_estimate=cost(20 * map_rows * frames * line, 6 * map_rows * frames * line, map_rows * frames * line),
        name="decode",
    )(feat, grad, scale, shift, film_scale, film_shift)


def blocks_to_lanes(values, rows):
    return jnp.concatenate([values[s : s + rows] for s in range(0, values.shape[0], rows)], axis=1)


def put(own_ref, other_ref, core, start, values):
    size, lanes = own_ref.shape[0], slice(start, start + values.shape[1])
    low = values.astype(BF)
    first = core == 0
    own_ref[:, lanes] = jnp.where(first, low[:size], low[size:])
    other_ref[:, lanes] = jnp.where(first, low[size:], low[:size])


def heads_kernel(
    place_ref, state_ref, cot_ref, live_ref, prior_ref, scale_grad_ref, shift_grad_ref, own_out, other_out,
    stream_out,
):
    live = live_ref[:, :1]
    grad = (cot_ref[...].astype(F32) * live).astype(BF)
    size = 2 * own_out.shape[0]
    core = place_ref[1]
    logits = grad.shape[1]
    state = state_ref[...]
    model = state.shape[1]
    start = pl.multiple_of(place_ref[0] * size, size)
    put(own_out, other_out, core, 0, tn(state_ref[:, pl.ds(start, size)], grad))
    stream_out[...] = nt(grad, prior_ref[...])
    scale_grad = nn(scale_grad_ref[...], state)
    blank = jnp.zeros((size - scale_grad.shape[0], model), F32)
    put(own_out, other_out, core, logits, jnp.concatenate([scale_grad, blank], axis=0))
    put(own_out, other_out, core, logits + model, blocks_to_lanes(nn(shift_grad_ref[...], state), size))


def heads(place, parts, state, logit_cot, live_cols, prior_w, scale_grad, shift_grad):
    frames, model = state.shape
    logits = logit_cot.shape[1]
    size = model // parts
    width = logits + model + shift_grad.shape[0] // size * model
    vmem = pl.BlockSpec(memory_space=pltpu.VMEM)
    return pl.pallas_call(
        heads_kernel,
        in_specs=[pl.BlockSpec(memory_space=pltpu.SMEM)] + [vmem] * 6,
        out_shape=[jax.ShapeDtypeStruct((size // 2, width), BF)] * 2
        + [jax.ShapeDtypeStruct((frames, model), F32)],
        compiler_params=params(60),
        cost_estimate=cost(4 * frames * model * logits, 4 * 1024 * 1024),
        name="heads",
    )(place, state, logit_cot, live_cols, prior_w, scale_grad, shift_grad)


def norm_backward(grad, unit, inverse):
    return (
        grad
        - jnp.mean(grad, axis=-1, keepdims=True)
        - unit * jnp.mean(grad * unit, axis=-1, keepdims=True)
    ) * inverse


def block_backward_kernel(
    columns, place_ref, part_ref, more_ref, embed_part_ref, embed_more_ref, stream_ref, ln1_ref, ln2_ref,
    down_in, slope_in, active_in, middle_in, up_in, context_in, out_in, joined_in, attend_in, qkv_in, emb_in,
    profile_in, own_out, other_out, profile_out, down_ref, slope_ref, active_ref, middle_ref, up_ref, context_ref, out_ref,
    joined_ref, attend_ref, qkv_ref, emb_ref, profile_ref, raised_scr, low_scr, grad_scr, in_sems,
):
    names = ("down", "slope", "active", "middle", "up", "context", "out", "joined", "attend", "qkv", "emb", "profile")
    sources = (
        down_in, slope_in, active_in, middle_in, up_in, context_in, out_in, joined_in, attend_in, qkv_in, emb_in,
        profile_in,
    )
    targets = (
        down_ref, slope_ref, active_ref, middle_ref, up_ref, context_ref, out_ref, joined_ref, attend_ref, qkv_ref,
        emb_ref, profile_ref,
    )
    copies = dict(zip(names, fetch(sources, targets, in_sems)))
    grad_out = stream_ref[...] + part_ref[...].astype(F32) + more_ref[...].astype(F32)
    frames, model = grad_out.shape
    hidden = up_ref.shape[1]
    branch = grad_out.astype(BF)
    place, core = place_ref[0], place_ref[1]
    size = 2 * own_out.shape[0]
    start_qkv, start_out, start_down = hidden, hidden + 3 * model, hidden + 4 * model
    start_norm = start_down + hidden // model * model
    copies["down"].wait()
    copies["slope"].wait()
    for start in range(0, hidden, 512):
        lanes = slice(start, start + 512)
        raised_scr[:, lanes] = (nt(branch, down_ref[lanes, :]) * slope_ref[:, lanes].astype(F32)).astype(BF)
    copies["active"].wait()
    for s in range(0, hidden, model):
        some = active_ref[:, pl.ds(pl.multiple_of(place * size + s, size), size)]
        put(own_out, other_out, core, start_down + s, tn(some, branch))
    copies["middle"].wait()
    middle = middle_ref[...]
    unit, inverse = normed(middle)
    low_scr[...] = (unit * ln2_ref[...]).astype(BF)
    window = pl.ds(pl.multiple_of(place * size, size), size)
    put(own_out, other_out, core, 0, tn(low_scr[:, window], raised_scr[...]))
    copies["up"].wait()
    grad = nt(raised_scr[...], up_ref[...])
    norm_two = jnp.sum(grad * unit, axis=0, keepdims=True)
    grad_middle = grad_out + norm_backward(grad * ln2_ref[...], unit, inverse)
    attended = grad_middle.astype(BF)
    copies["context"].wait()
    put(own_out, other_out, core, start_out, tn(context_ref[:, window], attended))
    copies["out"].wait()
    low_scr[...] = nt(attended, out_ref[...]).astype(BF)
    block = 128
    col = lax.broadcasted_iota(jnp.int32, (block, block), 1)
    first = col < 64
    scaling = 1.0 / math.sqrt(model // HEADS)
    copies["joined"].wait()
    copies["attend"].wait()
    for b in range(frames // block):
        part = slice(b * block, (b + 1) * block)
        for pair in range(HEADS // 2):
            lanes = pair * 128
            queries = joined_ref[part, lanes : lanes + 128]
            keys = stacked_heads(joined_ref[part, model + lanes : model + lanes + 128], col)
            values = stacked_heads(joined_ref[part, 2 * model + lanes : 2 * model + lanes + 128], col)
            grads = low_scr[part, lanes : lanes + 128]
            weights_low = attend_ref[b * HEADS // 2 + pair]
            weights = weights_low.astype(F32)
            terms = weights * nt(grads, values)
            halves = []
            for half in range(2):
                some = slice(half * block, (half + 1) * block)
                inner = jnp.sum(terms[:, some], axis=-1, keepdims=True)
                halves.append((terms[:, some] - weights[:, some] * inner).astype(BF))
            grad_scores = jnp.concatenate(halves, axis=1)
            grad_queries = nn(grad_scores, keys)
            both = tn(grad_scores, queries)
            grad_keys = jnp.where(first, both[:block], both[block:])
            both = tn(weights_low, grads)
            grad_values = jnp.where(first, both[:block], both[block:])
            for k, term in enumerate((grad_queries * scaling, grad_keys * scaling, grad_values)):
                grad_scr[part, k * model + lanes : k * model + lanes + 128] = term.astype(BF)
    unit, inverse = normed(embed_part_ref[...].astype(F32) + embed_more_ref[...].astype(F32))
    low_scr[...] = (unit * ln1_ref[...]).astype(BF)
    put(own_out, other_out, core, start_qkv, tn(low_scr[:, window], grad_scr[...]))
    copies["qkv"].wait()
    grad = nt(grad_scr[...], qkv_ref[...])
    norm_one = jnp.sum(grad * unit, axis=0, keepdims=True)
    lines = [norm[:, s : s + 128] for norm in (norm_one, norm_two) for s in range(0, model, 128)]
    lines.append(jnp.zeros((size - len(lines), 128), F32))
    put(own_out, other_out, core, start_norm, jnp.concatenate(lines, axis=0))
    grad_embed = (grad_middle + norm_backward(grad * ln1_ref[...], unit, inverse)).astype(BF)
    copies["emb"].wait()
    profile_out[...] = nt(emb_ref[...], grad_embed) * (1.0 / columns)
    copies["profile"].wait()
    put(own_out, other_out, core, start_norm + 128, blocks_to_lanes(nn(profile_ref[...], grad_embed), size))


def block_backward(
    columns, parts, place, grads, embeds, stream, joined, attend, context, middle, active, slope, profile,
    ln1, qkv, out_w, ln2, up_w, down_w, emb,
):
    frames, model = stream.shape
    hidden = up_w.shape[1]
    size = model // parts
    width = 2 * hidden + 4 * model + 128 + emb.shape[0] // size * model
    shapes = [((size // 2, width), BF), ((size // 2, width), BF), (profile.shape, F32)]
    vmem, hbm = pl.BlockSpec(memory_space=pltpu.VMEM), pl.BlockSpec(memory_space=pl.ANY)
    near = (*grads, *embeds, stream, ln1, ln2)
    staged = (down_w, slope, active, middle, up_w, context, out_w, joined, attend, qkv, emb, profile)
    return pl.pallas_call(
        functools.partial(block_backward_kernel, columns),
        in_specs=[pl.BlockSpec(memory_space=pltpu.SMEM)] + [vmem] * len(near) + [hbm] * len(staged),
        out_shape=[jax.ShapeDtypeStruct(*s) for s in shapes],
        scratch_shapes=[pltpu.VMEM(x.shape, x.dtype) for x in staged]
        + [
            pltpu.VMEM((frames, hidden), BF),
            pltpu.VMEM((frames, model), BF),
            pltpu.VMEM((frames, 3 * model), BF),
            pltpu.SemaphoreType.DMA((len(staged),)),
        ],
        compiler_params=params(60),
        cost_estimate=cost(3 * frames * model * (4 * model + 2 * hidden), 20 * 1024 * 1024),
        name="block_backward",
    )(place, *near, *staged)


def scatter_body(
    step, last, row_refs, first_ref, up_ref, down_ref, live, matrix_ref, places_ref, outs, scrs, fill
):
    rows_out, rim_up_out, rim_down_out, taps_out = outs
    ring_scr, window_scr, low_scr, rows_scr, held_scr, cov_scr = scrs
    _, lanes, frames = up_ref.shape
    depth, _ = matrix_ref.shape
    stride = lanes // GROUPS
    inner = slice(PAD, PAD + lanes)
    kind = rows_out.dtype

    @pl.when(step == 0)
    def _():
        cov_scr[...] = jnp.zeros_like(cov_scr)
        rows_scr[...] = jnp.zeros_like(rows_scr)
        held_scr[...] = jnp.zeros_like(held_scr)

    rows_out[0:3] = held_scr[...]

    @pl.when(step < last)
    def _():
        fill_six(
            ring_scr, step == 0, step == last - 1, (lambda: up_ref[0], lambda: first_ref[0]), row_refs, down_ref,
            live,
        )
        matrix = matrix_ref[...]
        for r in range(2):
            fill_windows_at(window_scr, ring_scr, 2 * r, depth // SLOT, stride)
            fill(r)
            placed = nn(matrix, low_scr[...])
            for g in range(GROUPS):
                add_rows(rows_scr, 2 * r, placed[:, g * frames : (g + 1) * frames], g, stride)
            cov_scr[...] += nt(low_scr[...], window_scr[...])

    rows_out[3] = rows_scr[0, inner, :].astype(kind)

    @pl.when(step == 0)
    def _():
        rim_up_out[...] = rows_scr[0, inner, :].astype(BF)

    @pl.when(step == last)
    def _():
        rim_down_out[...] = rows_scr[1, inner, :].astype(BF)
        taps_out[...] = fold_taps(cov_scr, places_ref, taps_out.shape[1])

    @pl.when(step < last)
    def _():
        held_scr[...] = rows_scr[1:4, inner, :].astype(kind)
        rows_scr[0:2] = rows_scr[4:6]
        rows_scr[2:6] = jnp.zeros((4,) + rows_scr.shape[1:], F32)


def rebuild_kernel(
    feat_ref, a_ref, b_ref, c_ref, d_ref, first_ref, up_ref, down_ref, live_ref, dec_ref, scale_ref, shift_ref,
    places_ref, rows_out, rim_up_out, rim_down_out, taps_out,
    ring_scr, window_scr, low_scr, rows_scr, held_scr, cov_scr,
):
    frames = up_ref.shape[2]
    width = dec_ref.shape[1]
    channels = scale_ref.shape[0]

    def fill(r):
        scale = (scale_ref[...] * 0.5).astype(BF)
        shift = (shift_ref[r * channels : (r + 1) * channels, :] * 0.5).astype(BF)
        for g in range(GROUPS):
            for tile, column in tiles(frames, g):
                for j in range(0, width, channels):
                    feat = feat_ref[r, g * width + j : g * width + j + channels, tile]
                    low_scr[j : j + channels, column] = gelu_of_half(feat * scale[:, tile] + shift[:, tile])

    scatter_body(
        pl.program_id(0), pl.num_programs(0) - 1, (a_ref, b_ref, c_ref, d_ref), first_ref, up_ref, down_ref,
        live_ref[...], dec_ref, places_ref, (rows_out, rim_up_out, rim_down_out, taps_out),
        (ring_scr, window_scr, low_scr, rows_scr, held_scr, cov_scr), fill,
    )


def encode_backward_kernel(
    back_ref, a_ref, b_ref, c_ref, d_ref, first_ref, up_ref, down_ref, enc_cols_ref, enc_ref, scale_ref, profile_ref,
    places_ref, rows_out, rim_up_out, rim_down_out, taps_out,
    ring_scr, window_scr, low_scr, rows_scr, held_scr, cov_scr, value_scr,
):
    frames = up_ref.shape[2]
    width = enc_ref.shape[1]
    channels = scale_ref.shape[0]

    def fill(r):
        value_scr[...] = nn(enc_cols_ref[...], window_scr[...])
        scale = (scale_ref[...] * 0.5).astype(BF)
        mean = (profile_ref[r * channels : (r + 1) * channels, :] * 0.5).astype(BF)
        for g in range(GROUPS):
            for tile, column in tiles(frames, g):
                for j in range(0, width, channels):
                    back = back_ref[r, g * width + j : g * width + j + channels, tile]
                    slope = double_slope((value_scr[j : j + channels, column] * SHRINK).astype(BF))
                    low_scr[j : j + channels, column] = (back * scale[:, tile] + mean[:, tile]) * slope

    scatter_body(
        pl.program_id(0), pl.num_programs(0) - 1, (a_ref, b_ref, c_ref, d_ref), first_ref, up_ref, down_ref,
        None, enc_ref, places_ref, (rows_out, rim_up_out, rim_down_out, taps_out),
        (ring_scr, window_scr, low_scr, rows_scr, held_scr, cov_scr), fill,
    )


def scatter_call(kernel, name, kind, which, map_in, rows_in, up, down, more, more_specs, width, depth, channels):
    rows, lanes, frames = rows_in.shape
    steps = rows // 4
    line = GROUPS * width
    rim = jax.ShapeDtypeStruct((lanes, frames), BF)
    taps = jax.ShapeDtypeStruct((more[-1].shape[1], channels), F32)
    scratch = [
        pltpu.VMEM((6, lanes + 2 * PAD, frames), BF),
        pltpu.VMEM((depth, GROUPS * frames), BF),
        pltpu.VMEM((width, GROUPS * frames), BF),
        pltpu.VMEM((6, lanes + 2 * PAD, frames), F32),
        pltpu.VMEM((3, lanes, frames), kind),
        pltpu.VMEM((width, depth), F32),
    ]
    if which == 0:
        scratch.append(pltpu.VMEM((width, GROUPS * frames), F32))
    return pl.pallas_call(
        kernel,
        grid=(steps + 1,),
        in_specs=[pl.BlockSpec((2, line, frames), lambda i: (jnp.minimum(i, steps - 1), 0, 0))]
        + four_row_specs(frames, lanes, rows)
        + [pl.BlockSpec((1, lanes, frames), lambda i: (0, 0, 0)), halo_spec(up, which), halo_spec(down, which)]
        + more_specs,
        out_specs=[
            pl.BlockSpec((4, lanes, frames), lambda i: (jnp.maximum(i - 1, 0), 0, 0)),
            whole(rim.shape),
            whole(rim.shape),
            whole(taps.shape),
        ],
        out_shape=[jax.ShapeDtypeStruct((rows, lanes, frames), kind), rim, rim, taps],
        scratch_shapes=scratch,
        compiler_params=params(60),
        cost_estimate=cost(4 * rows * frames * line * 128, 2 * rows * frames * line),
        name=name,
    )(map_in, *[rows_in] * 5, up, down, *more)


def row_block(channels, frames, rows):
    return pl.BlockSpec((2 * channels, frames), lambda i: (jnp.minimum(i, rows // 4 - 1), 0))


def rebuild(feat, recon_rows, up, down, live, dec, scale, shift, places):
    rows, _, frames = recon_rows.shape
    channels = scale.shape[0]
    return scatter_call(
        rebuild_kernel, "rebuild", BF, 1, feat, recon_rows, up, down, (live, dec, scale, shift, places),
        [whole(live.shape), whole(dec.shape), whole(scale.shape), row_block(channels, frames, rows), whole(places.shape)],
        dec.shape[1], dec.shape[0], channels,
    )


def encode_backward(back, image_rows, up, down, enc_cols, enc, scale, profile, places):
    rows, _, frames = image_rows.shape
    channels = scale.shape[0]
    return scatter_call(
        encode_backward_kernel, "encode_backward", F32, 0, back, image_rows, up, down,
        (enc_cols, enc, scale, profile, places),
        [
            whole(enc_cols.shape), whole(enc.shape), whole(scale.shape), row_block(channels, frames, rows),
            whole(places.shape),
        ],
        enc.shape[1], enc.shape[0], channels,
    )


def rims_kernel(low_ref, wide_ref, above_ref, below_ref, low_out, wide_out):
    for at, rim_ref in ((0, above_ref), (1, below_ref)):

        @pl.when(pl.program_id(0) == at)
        def _(rim_ref=rim_ref):
            for k, (rows_ref, out_ref) in enumerate(((low_ref, low_out), (wide_ref, wide_out))):
                out_ref[0] = (rows_ref[0].astype(F32) + rim_ref[k].astype(F32)).astype(out_ref.dtype)


def with_rims(low, wide, above, below):
    count, lanes, frames = low.shape
    row_spec = pl.BlockSpec((1, lanes, frames), lambda i: (i * (count - 1), 0, 0))
    return pl.pallas_call(
        rims_kernel,
        grid=(2,),
        in_specs=[row_spec, row_spec, whole(above.shape), whole(below.shape)],
        out_specs=[row_spec, row_spec],
        out_shape=[jax.ShapeDtypeStruct(low.shape, low.dtype), jax.ShapeDtypeStruct(wide.shape, wide.dtype)],
        input_output_aliases={0: 0, 1: 1},
        compiler_params=params(60),
        cost_estimate=cost(0, 16 * lanes * frames),
        name="with_rims",
    )(low, wide, above, below)


def send_along(values, axis, step):
    count = lax.axis_size(axis)
    pairs = [(i, i + step) for i in range(count) if 0 <= i + step < count]
    return lax.ppermute(values, axis, pairs)


def swap(values, axis, distance):
    count = lax.axis_size(axis)
    return lax.ppermute(values, axis, [(i, i ^ distance) for i in range(count)])


def cross(values, turn):
    rows, frames = lax.axis_size("rows"), lax.axis_size("frames")
    pairs = []
    for r in range(rows):
        for f in range(frames):
            distance = 1 + (f + turn) % 2
            pairs.append((r * frames + f, (r ^ distance) * frames + f))
    return lax.ppermute(values, ("rows", "frames"), pairs)


def add(values, more):
    return (values.astype(F32) + more.astype(F32)).astype(BF)


def chip_groups():
    count = lax.axis_size("frames")
    return [list(range(core, count, 2)) for core in range(2)]


def split_over(values, groups):
    count = len(groups[0])
    split = values.reshape((count, values.shape[0] // count) + values.shape[1:])
    return lax.all_to_all(split, "frames", 0, 0, axis_index_groups=groups)


def sum_parts(parts):
    return jnp.sum(parts.astype(F32), axis=0).astype(BF)


def gather_over(values, axis):
    count = lax.axis_size(axis)
    copies = jnp.broadcast_to(values[None], (count,) + values.shape)
    return lax.all_to_all(copies, axis, 0, 0)


def swap_frames(values, distance):
    count = lax.axis_size("frames")
    return lax.ppermute(values, "frames", [(f, f ^ distance) for f in range(count)])


def gather_chips(values):
    count = lax.axis_size("frames") // 2
    copies = jnp.broadcast_to(values[None], (count,) + values.shape)
    return lax.all_to_all(copies, "frames", 0, 0, axis_index_groups=chip_groups())


def finish_kernel(slots, widths, place_ref, *refs):
    count = len(slots)
    own_in, other_in = refs[:count], refs[count : 2 * count]
    outs, (own_scr, other_scr, sems) = refs[-10:-3], refs[-3:]
    scale_before = refs[-11]
    step = pl.program_id(0)
    core = place_ref[4]
    chips = own_scr.shape[1]
    copies = [
        [pltpu.make_async_copy(ref, scr.at[k], sems.at[side, k]) for k, ref in enumerate(sources)]
        for side, (sources, scr) in enumerate(((own_in, own_scr), (other_in, other_scr)))
    ]

    @pl.when(step == 0)
    def _():
        for k in range(count):
            copies[0][k].start()
            copies[1][k].start()

    for k in range(count):

        @pl.when(step == k)
        def _(k=k):
            copies[0][k].wait()
            copies[1][k].wait()
            for scr, half in ((own_scr, core), (other_scr, 1 - core)):
                for chip in range(chips):
                    at, piece = 0, half * chips + chip
                    for out, (kind, lanes) in zip(outs, widths):
                        part = scr[k, chip, :, at : at + lanes].astype(F32)
                        at += lanes
                        if kind == "row":
                            out[piece] = part
                        elif kind == "blocks":
                            size = out.shape[-1]
                            for block in range(out.shape[0]):
                                out[block, piece] = part[:, block * size : (block + 1) * size]
                        elif kind == "norm" and k == 0:
                            out[piece] = part
                        elif kind == "scale":
                            if k:
                                out[piece] += part
                            else:
                                out[piece] = part + scale_before[piece] if slots[0] else part


def finish(place, slots, own, other, before, logits, model, hidden):
    chips, size, lanes = own[0].shape
    pieces = 2 * chips
    quarters = 4
    many = hidden // model
    widths = (
        ("row", logits), ("scale", model), ("row", hidden), ("row", 3 * model), ("row", model), ("blocks", hidden),
        ("norm", 128),
    )
    specs, shapes = [], []
    for kind, width in widths:
        if kind == "blocks":
            shape, index = (many, pieces, size, model), lambda k, place: (0, place[slots[0] + k], 0, 0)
            shapes.append((many, quarters * pieces, size, model))
        elif kind == "row":
            shape, index = (pieces, size, width), lambda k, place: (place[slots[0] + k], 0, 0)
            shapes.append((quarters * pieces, size, width))
        else:
            shape, index = (pieces, size, width), lambda k, place: (0, 0, 0)
            shapes.append(shape)
        specs.append(pl.BlockSpec(shape, index))
    held = pltpu.VMEM((len(slots), chips, size, lanes), BF)
    arrays = len(own) + len(other)
    kept = [k for k, (kind, _) in enumerate(widths) if kind in ("row", "blocks")]
    more = [before[k] for k in kept] + [before[1]] if before else [jnp.zeros((1, 8, 128), F32)]
    return pl.pallas_call(
        functools.partial(finish_kernel, slots, widths),
        grid_spec=pltpu.PrefetchScalarGridSpec(
            num_scalar_prefetch=1,
            grid=(len(slots),),
            in_specs=[pl.BlockSpec(memory_space=pl.ANY)] * (arrays + len(more) - 1) + [whole(more[-1].shape)],
            out_specs=specs,
            scratch_shapes=[held, held, pltpu.SemaphoreType.DMA((2, len(slots)))],
        ),
        out_shape=[jax.ShapeDtypeStruct(shape, F32) for shape in shapes],
        input_output_aliases={1 + arrays + n: k for n, k in enumerate(kept)} if before else {},
        compiler_params=params(60),
        cost_estimate=cost(0, 10 * len(slots) * own[0].size),
        name="finish",
    )(place, *own, *other, *more)


def split_finish_kernel(place_ref, split_ref, split_other_ref, *outs):
    core = place_ref[4]
    chips = split_ref.shape[0]
    pieces = 2 * chips
    for ref, half in ((split_ref, core), (split_other_ref, 1 - core)):
        for chip in range(chips):
            at = 0
            for out in outs:
                lanes = out.shape[-1]
                for block in range(out.shape[0] // pieces):
                    out[block * pieces + half * chips + chip] = ref[chip, :, at : at + lanes].astype(F32)
                    at += lanes


def split_finish(place, split, split_other, model):
    chips, size, lanes = split.shape
    shape = (lanes // (2 * model) * 2 * chips, size, model)
    vmem = pl.BlockSpec(memory_space=pltpu.VMEM)
    return pl.pallas_call(
        split_finish_kernel,
        in_specs=[pl.BlockSpec(memory_space=pltpu.SMEM), vmem, vmem],
        out_shape=[jax.ShapeDtypeStruct(shape, F32)] * 2,
        compiler_params=params(40),
        cost_estimate=cost(0, 8 * split.size),
        name="split_finish",
    )(place, split, split_other)


def on_device(
    images, enc_kernel, emb_weight, ln1_gain, qkv_weight, out_weight, ln2_gain, up_weight, down_weight,
    prior_weight, film_scale, film_shift, dec_kernel, horizons, frame_valid, recon_cot, logit_cot,
):
    frames, rows, lanes = images.shape
    taps, _, chan_in, channels = enc_kernel.shape
    columns = lanes // chan_in // 2
    copies = columns // GROUPS
    model = qkv_weight.shape[0]
    hidden = up_weight.shape[1]
    slots = frames // horizons.shape[0]
    count = lax.axis_size("rows")

    places = jnp.asarray(tap_places(taps, chan_in, copies), BF)
    enc_taps = jnp.transpose(enc_kernel, (0, 2, 1, 3)).reshape(taps * chan_in * taps, channels)
    dec_taps = jnp.transpose(dec_kernel, (0, 3, 1, 2)).reshape(taps * chan_in * taps, channels)
    film_scale_rows = film_scale.T
    image_rows = jnp.transpose(images, (1, 2, 0))
    recon_rows = jnp.transpose(recon_cot, (1, 2, 0))

    steps = jnp.arange(slots)
    reached = (steps[None, :] <= horizons[:, None]).reshape(frames)
    live = (reached & (frame_valid > 0)).astype(F32)
    live_cols = jnp.broadcast_to(live[:, None], (frames, 128))
    keys_ok = reached.astype(F32)[None, :]
    place = jnp.stack([lax.axis_index("rows"), lax.axis_index("frames") % 2]).astype(jnp.int32)

    above = send_along(jnp.stack([image_rows[-1], recon_rows[-1]]), "rows", 1)
    below = send_along(jnp.stack([image_rows[0], recon_rows[0]]), "rows", -1)
    enc_cols, enc, dec_cols, dec = expand(enc_taps, dec_taps, places)

    feat, inner = encode_inner(image_rows, enc_cols, channels)
    feat, profile, embed_part = encode_edge(image_rows, above, below, enc_cols, emb_weight, inner, feat)
    recon_later, embed_part = lax.optimization_barrier((recon_rows, embed_part))
    embed_more = cross(embed_part, 0)
    half = rows // 8
    decoded_args = (recon_later, above, below, live[None, :], dec_cols)
    grad = decoded_grad(*decoded_args, 0, half, ())
    embed_more, grad = lax.optimization_barrier((embed_more, grad))
    embed_part = add(embed_part, embed_more)
    embed_more = cross(embed_part, 1)
    grad = decoded_grad(*decoded_args, half, rows // 4 - half, (grad,))
    embed_more, grad = lax.optimization_barrier((embed_more, grad))
    embeds = embed_part, embed_more
    joined, attend, context, middle, active, active_slope, state, scale, shift = block_forward(
        slots, embeds, keys_ok, ln1_gain[None], qkv_weight, out_weight, ln2_gain[None], up_weight, down_weight,
        film_scale_rows, film_shift,
    )
    back, scale_grad, shift_grad, film_part = decode(feat, grad, scale, shift, film_scale_rows, film_shift)
    film_more = cross(film_part, 0)
    head_own, head_other, stream = heads(place, count, state, logit_cot, live_cols, prior_weight, scale_grad, shift_grad)
    film_more, head_other = lax.optimization_barrier((film_more, head_other))
    film_part = add(film_part, film_more)
    film_more = cross(film_part, 1)
    head_half_sum = add(head_own, swap_frames(head_other, 1))
    film_more, head_half_sum = lax.optimization_barrier((film_more, head_half_sum))
    head_parts = split_over(head_half_sum, chip_groups())
    block_own, block_other, grad_profile = block_backward(
        columns, count, place, (film_part, film_more), embeds, stream, joined, attend, context, middle, active,
        active_slope, profile, ln1_gain[None], qkv_weight, out_weight, ln2_gain[None], up_weight, down_weight,
        emb_weight,
    )
    head_parts, block_other = lax.optimization_barrier((head_parts, block_other))
    head_piece = sum_parts(head_parts)
    logits = prior_weight.shape[1]
    head_lanes, block_lanes = logits + model, 2 * hidden + 4 * model + 128
    block_more = swap_frames(block_other, 1)
    block_half_sum = add(block_own, block_more)
    feat, block_half_sum = lax.optimization_barrier((feat, block_half_sum))
    block_parts = split_over(block_half_sum, chip_groups())
    rebuilt_rows, rim_up, rim_down, dec_cov = rebuild(
        feat, recon_rows, above, below, live[None, :], dec, scale, shift, places
    )
    block_parts, dec_cov = lax.optimization_barrier((block_parts, dec_cov))
    block_piece = sum_parts(block_parts)
    shared = jnp.concatenate([head_piece[:, :head_lanes], block_piece[:, :block_lanes]], axis=1)
    shared, back = lax.optimization_barrier((shared, back))
    own = gather_chips(shared)
    image_grad, image_up, image_down, enc_cov = encode_backward(
        back, image_rows, above, below, enc_cols, enc, scale, grad_profile, places
    )
    own, enc_cov = lax.optimization_barrier((own, enc_cov))
    near, far, own_other = cross(own, 0), cross(own, 1), swap_frames(own, 1)
    covs = jnp.concatenate([enc_cov, dec_cov], axis=1)
    step = lax.axis_size("frames") // 2
    while step:
        covs = covs + swap_frames(covs, step)
        step //= 2
    row, core = lax.axis_index("rows"), lax.axis_index("frames") % 2
    slots_of = jnp.stack([row, row ^ (1 + core), row ^ (2 - core), row ^ 3, core]).astype(jnp.int32)
    split = gather_chips(jnp.concatenate([head_piece[:, head_lanes:], block_piece[:, block_lanes:]], axis=1))
    near, far, own_other, covs, split = lax.optimization_barrier((near, far, own_other, covs, split))
    both = cross(near, 1)
    near_other, far_other = swap_frames(near, 1), swap_frames(far, 1)
    found = finish(
        slots_of, (0, 1, 2), (own, near, far), (own_other, far_other, near_other), (), logits, model, hidden
    )
    film_shift_grad, emb_grad = split_finish(slots_of, split, swap_frames(split, 1), model)
    film_shift_grad = film_shift_grad.reshape(-1, model).T
    emb_grad = emb_grad.reshape(-1, model)
    norm_grads = found[6].reshape(-1, 128)[: 2 * model // 128].reshape(2, model)
    rims = jnp.stack([rim_down, image_down]), jnp.stack([rim_up, image_up])
    both, covs, rims, film_shift_grad, emb_grad, norm_grads, *found = lax.optimization_barrier(
        (both, covs, rims, film_shift_grad, emb_grad, norm_grads, *found)
    )
    both_other = swap_frames(both, 1)
    rims_above, rims_below = send_along(rims[0], "rows", 1), send_along(rims[1], "rows", -1)
    for distance in (1, 2):
        covs = covs + lax.ppermute(covs, "rows", [(r, r ^ distance) for r in range(count)])
    found = finish(slots_of, (3,), (both,), (both_other,), found, logits, model, hidden)
    prior_grad, misc, up_grad, qkv_grad, out_grad, down_grad = [
        array.reshape(-1, array.shape[-1]) for array in found[:6]
    ]
    film_scale_grad = misc[:channels].T
    rims_above, rims_below, film_scale_grad, prior_grad = lax.optimization_barrier(
        (rims_above, rims_below, film_scale_grad, prior_grad)
    )
    rebuilt_rows, image_grad = with_rims(rebuilt_rows, image_grad, rims_above, rims_below)
    enc_cov, dec_cov = covs[:, :channels], covs[:, channels:]
    enc_grad = jnp.transpose(enc_cov.reshape(taps, chan_in, taps, channels), (0, 2, 1, 3))
    dec_grad = jnp.transpose(dec_cov.reshape(taps, chan_in, taps, channels), (0, 2, 3, 1))
    return (
        jnp.transpose(rebuilt_rows, (2, 0, 1)),
        jnp.transpose(image_grad, (2, 0, 1)),
        enc_grad,
        emb_grad,
        norm_grads[0],
        qkv_grad,
        out_grad,
        norm_grads[1],
        up_grad,
        down_grad,
        prior_grad,
        film_scale_grad,
        film_shift_grad,
        dec_grad,
    )


def solution(mesh):
    return jax.shard_map(
        on_device,
        mesh=mesh,
        in_specs=(
            P("frames", "rows", None),
            P(),
            P("rows", None),
            P(),
            P(),
            P(),
            P(),
            P(),
            P(),
            P(),
            P(),
            P(None, "rows"),
            P(),
            P("frames"),
            P("frames"),
            P("frames", "rows", None),
            P("frames", None),
        ),
        out_specs=(
            P("frames", "rows", None),
            P("frames", "rows", None),
            P(),
            P("rows", None),
            P(),
            P(),
            P(),
            P(),
            P(),
            P(),
            P(),
            P(),
            P(None, "rows"),
            P(),
        ),
        check_vma=False,
    )
```

time: 750 us -> 237 us (0.32)
  matrix products: 240 us -> 0 us
  local copies, waits for them, and re-layouts: 243 us -> 14.2 us
  Pallas kernels: 0 us -> 127 us
  other arithmetic: 99.2 us -> 8.15 us
  blocking collectives: 53.5 us -> 0 us
  waiting for transfers between devices: 65.1 us -> 40.7 us
  starting transfers between devices: 27.4 us -> 45.3 us
  between operations: 14.9 us -> 1.03 us
    dot_general x40 -> x0, matrix products: 157 us -> none  [the longest x36 131 us: product(): jnp.einsum(pattern, lhs_array, rhs_array, preferred_element_type=jnp.floa...]
    pallas_call x0 -> x15, Pallas kernels: none -> 127 us  [the longest x2 38.2 us: scatter_call(): pl.pallas_call(kernel, grid=(steps + 1,), in_specs=[pl.BlockSpec((2, line...]
    another operation x13 -> x1, local copies, waits for them, and re-layouts: 81.5 us -> 0.08 us  [on_device(): jnp.stack([row, row ^ 1 + core, row ^ 2 - core, row ^ 3, core])]
    psum x4 -> x0, waiting for transfers between devices: 65 us -> none  [the longest x1 39.1 us: on_device(): lax.psum(grad_film.astype(jnp.bfloat16), 'rows').astype(jnp.float32)]
    psum x2 -> x0, blocking collectives: 53.5 us -> none  [the longest x1 38.1 us: on_device(): lax.psum((enc_kernel_grad, dec_kernel_grad, film_scale_grad), ('rows', 'f...]
    slice x18 -> x8, local copies, waits for them, and re-layouts: 57.4 us -> 4.72 us  [the longest x1 1.54 us: on_device(): film_scale_grad = misc[:channels].T]
    pad x3 -> x0, matrix products: 49.4 us -> none  [pad_rows(): return jnp.pad(values, ((0, 0), (before, after), (0, 0)))]
    convert_element_type x13 -> x6, other arithmetic: 53 us -> 4.53 us  [the longest x4 4.45 us: add(): return (values.astype(F32) + more.astype(F32)).astype(BF)]
  transfers between devices with their start and end apart: 12 -> 27, of which waited for: 2 -> 14; matrix products, arithmetic and copies ran while one was open for 60% -> 6% of each run, Pallas kernels for 0% -> 39%
where the time goes in v1:
time: 237 us; the launch traced here: 236 us
  Pallas kernels  127 us (54%)
  starting transfers between devices  45.3 us (19%)
  waiting for transfers between devices  40.7 us (17%)
  local copies, waits for them, and re-layouts  14.2 us (6%)
  other arithmetic  8.15 us (3%)
    pallas_call x2, Pallas kernels, scatter_call(): pl.pallas_call(kernel, grid=(steps + 1,), in_specs=[pl.BlockSpec((2, line...  38.2 us
    ppermute x10, waiting for transfers between devices, swap_frames(): lax.ppermute(values, 'frames', [(f, f ^ distance) for f in range(count)])  19.2 us
    pallas_call x1, Pallas kernels, decode(): pl.pallas_call(decode_kernel, grid=(map_rows // 2,), in_specs=[map_spec,...  16.9 us
    pallas_call x1, Pallas kernels, block_backward(): pl.pallas_call(functools.partial(block_backward_kernel, columns), in_spec...  15.4 us
    pallas_call x2, Pallas kernels, finish(): pl.pallas_call(functools.partial(finish_kernel, slots, widths), grid_spec...  12.6 us
    ppermute x4, starting transfers between devices, send_along(): return lax.ppermute(values, axis, pairs)  9.97 us
    pallas_call x2, Pallas kernels, decoded_grad(): pl.pallas_call(functools.partial(decoded_grad_kernel, base, map_rows // 2...  9.97 us
    all_to_all x2, starting transfers between devices, split_over(): return lax.all_to_all(split, 'frames', 0, 0, axis_index_groups=groups)  9.94 us
  transfers between devices with their start and end apart: 27, of which 14 were waited for; matrix products, arithmetic and copies ran while one was open for 6% of the time, Pallas kernels for 39%

profile of v1, /device:TPU:0, one launch (start us, length us, event | category | flops | bytes accessed | tf_op | source)
XLA Modules:
  0.0 235.9 jit_solution(8560696478564757351)
XLA Ops:
  1.9 4.9 %collective-permute-start = (bf16[2,192,384]{2,1,0:T(8,128)(2,1)S(1)}, bf16[2,192,384]{2,1,0:T(8,128)(2,1)S(1)}, u32[]{:S(2)}, u32[]{:S(2)}) collective-permute-start(bf16[2,192,384]{2,1,0:T(8,128)(2,1)S(1)} %pad_maximum_fusion), channel_id=1, source_target_pairs={{0,8},{8,16},{16,24},{1,9},{9,17},{17,25},{2,10},{10,18},{18,26},{... | collective-permute-start | bytes 884744 | tf_op jit(solution)/shard_map/ppermute | solution.py:976
  8.1 2.1 expand.1
  10.2 8.7 %encode_inner.1 = (bf16[8,1536,384]{2,1,0:T(8,128)(2,1)}, bf16[288,384]{1,0:T(8,128)(2,1)}) custom-call(bf16[16,192,384]{2,1,0:T(8,128)(2,1)} %bitcast.63, bf16[16,192,384]{2,1,0:T(8,128)(2,1)} %bitcast.64, bf16[16,192,384]{2,1,0:T(8,128)(2,1)} %bitcast.65, bf16[16,192,384]{2,1,0:T(8,128)(2,1)} %bitcast.66, ...), custom_call_target="tpu_custom_call" | custom-call | flops 1811939328 | bytes 14155776 | tf_op jit(solution)/shard_map/encode_inner/pallas_call | solution.py:286
  18.9 2.3 collective-permute-done.1.down_ref
  22.0 5.1 %encode_edge.1 = (bf16[8,1536,384]{2,1,0:T(8,128)(2,1)}, bf16[384,384]{1,0:T(8,128)(2,1)}, bf16[384,512]{1,0:T(8,128)(2,1)}) custom-call(bf16[16,192,384]{2,1,0:T(8,128)(2,1)} %bitcast.67, bf16[16,192,384]{2,1,0:T(8,128)(2,1)} %bitcast.68, bf16[16,192,384]{2,1,0:T(8,128)(2,1)} %bitcast.69, ...), custom_call_target="tpu_custom_call", output_to_operand_aliasing={{0}: (8, {})} | custom-call | flops 603979776 | bytes 4718592 | tf_op jit(solution)/shard_map/encode_edge/pallas_call | solution.py:323
  29.3 5.0 %decoded_grad.2.rest_0_ = bf16[8,1536,384]{2,1,0:T(8,128)(2,1)} custom-call(bf16[16,192,384]{2,1,0:T(8,128)(2,1)} %bitcast.46, bf16[16,192,384]{2,1,0:T(8,128)(2,1)} %bitcast.47, bf16[16,192,384]{2,1,0:T(8,128)(2,1)} %bitcast.48, bf16[16,192,384]{2,1,0:T(8,128)(2,1)} %bitcast.49, bf16[2,192,384]{2,1,0:T(8,128)(2,1)} %copy-done.2, ...), custom_call_target="tpu_custom_call" | custom-call | flops 1207959552 | bytes 4718592 | tf_op jit(solution)/shard_map/decoded_grad/pallas_call | solution.py:500
  37.2 4.9 %decoded_grad.3.grad_ref = bf16[8,1536,384]{2,1,0:T(8,128)(2,1)} custom-call(bf16[16,192,384]{2,1,0:T(8,128)(2,1)} %bitcast.51, bf16[16,192,384]{2,1,0:T(8,128)(2,1)} %bitcast.52, bf16[16,192,384]{2,1,0:T(8,128)(2,1)} %bitcast.53, bf16[16,192,384]{2,1,0:T(8,128)(2,1)} %bitcast.54, bf16[16,192,384]{2,1,0:T(8,128)(2,1)} %bitcast.55, ...), custom_call_target="tpu_custom_call", output_to_operand_aliasing={{}: (9, {})} | custom-call | flops 1207959552 | bytes 4718592 | tf_op jit(solution)/shard_map/decoded_grad/pallas_call | solution.py:500
  43.8 9.7 %block_forward.1 = (bf16[384,1536]{1,0:T(8,128)(2,1)}, bf16[12,128,256]{2,1,0:T(8,128)(2,1)}, bf16[384,512]{1,0:T(8,128)(2,1)}, f32[384,512]{1,0:T(8,128)}, bf16...) custom-call(bf16[384,512]{1,0:T(8,128)(2,1)} %copy-done.4, ...), custom_call_target="tpu_custom_call" | custom-call | flops 2415919104 | bytes 16777216 | tf_op jit(solution)/shard_map/block_forward/pallas_call | solution.py:461
  53.5 16.9 %decode.1 = (bf16[8,1536,384]{2,1,0:T(8,128)(2,1)}, bf16[48,384]{1,0:T(8,128)(2,1)}, bf16[384,384]{1,0:T(8,128)(2,1)}, bf16[384,512]{1,0:T(8,128)(2,1)}) custom-call(bf16[8,1536,384]{2,1,0:T(8,128)(2,1)} %get-tuple-element.144.feat_ref, bf16[8,1536,384]{2,1,0:T(8,128)(2,1)} %decoded_grad.3.grad_ref, f32[48,384]{1,0:T(8,128)} %get-tuple-element.121.scale_ref, ...), custom_call_target="tpu_custom_call" | custom-call | flops 94371840 | bytes 28311552 | tf_op jit(solution)/shard_map/decode/pallas_call | solution.py:576
  73.4 4.0 %heads.1 = (bf16[64,3072]{1,0:T(8,128)(2,1)}, bf16[64,3072]{1,0:T(8,128)(2,1)}, f32[384,512]{1,0:T(8,128)}) custom-call(s32[2]{0:T(128)} %pad_add_fusion.place_ref, bf16[384,512]{1,0:T(8,128)(2,1)} %get-tuple-element.124.state_ref, bf16[384,1024]{1,0:T(8,128)(2,1)} %cot_ref.1, f32[384,128]{1,0:T(8,128)} %broadcast_in_dim.17.live_ref, ...), custom_call_target="tpu_custom_call" | custom-call | flops 805306368 | bytes 4194304 | tf_op jit(solution)/shard_map/heads/pallas_call | solution.py:637
  80.4 1.8 add_convert_fusion.1
  82.3 4.2 %collective-permute-done.5.more_ref = bf16[384,512]{1,0:T(8,128)(2,1)S(1)} collective-permute-done((bf16[384,512]{1,0:T(8,128)(2,1)S(1)}, bf16[384,512]{1,0:T(8,128)(2,1)S(1)}, u32[]{:S(2)}, u32[]{:S(2)}) %collective-permute-start.5) | collective-permute-done | bytes 393248 | tf_op jit(solution)/shard_map/ppermute | solution.py:991
  86.5 4.9 %all-to-all-start = ((bf16[4,16,3072]{2,1,0:T(8,128)(2,1)}), bf16[4,16,3072]{2,1,0:T(8,128)(2,1)S(1)}, u32[]{:S(2)}, u32[]{:S(2)}) async-start(bf16[4,16,3072]{2,1,0:T(8,128)(2,1)} %bitcast.11), calls=%async_computation | async-start | bytes 786432 | tf_op jit(solution)/shard_map/all_to_all | solution.py:1006
  91.4 15.4 %block_backward.1 = (bf16[64,7808]{1,0:T(8,128)(2,1)}, bf16[64,7808]{1,0:T(8,128)(2,1)}, f32[384,384]{1,0:T(8,128)}) custom-call(s32[2]{0:T(128)} %pad_add_fusion.place_ref, bf16[384,512]{1,0:T(8,128)(2,1)} %copy-done.5, bf16[384,512]{1,0:T(8,128)(2,1)} %copy-done.11, bf16[384,512]{1,0:T(8,128)(2,1)} %copy-done.4, bf16[384,512]{1,0:T(8,128)(2,1)} %copy-done.10, ...), custom_call_target="tpu_custom_call" | custom-call | flops 3623878656 | bytes 20971520 | tf_op jit(solution)/shard_map/block_backward/pallas_call | solution.py:762
  106.8 2.8 %collective-permute-done.7 = bf16[64,7808]{1,0:T(8,128)(2,1)S(1)} collective-permute-done((bf16[64,7808]{1,0:T(8,128)(2,1)}, bf16[64,7808]{1,0:T(8,128)(2,1)S(1)}, u32[]{:S(2)}, u32[]{:S(2)}) %collective-permute-start.7) | collective-permute-done | bytes 999456 | tf_op jit(solution)/shard_map/ppermute | solution.py:1021
  109.6 2.4 %add_convert_fusion = bf16[64,7808]{1,0:T(8,128)(2,1)} fusion(bf16[64,7808]{1,0:T(8,128)(2,1)S(1)} %collective-permute-done.7, bf16[64,7808]{1,0:T(8,128)(2,1)} %get-tuple-element.140), kind=kLoop, calls=%fused_computation | loop fusion | flops 1998848 | bytes 2998272 | tf_op jit(solution)/shard_map/convert_element_type | solution.py:995
  112.0 5.1 %all-to-all-start.1 = ((bf16[4,16,7808]{2,1,0:T(8,128)(2,1)}), bf16[4,16,7808]{2,1,0:T(8,128)(2,1)S(1)}, u32[]{:S(2)}, u32[]{:S(2)}) async-start(bf16[4,16,7808]{2,1,0:T(8,128)(2,1)} %bitcast.12), calls=%async_computation.1 | async-start | bytes 1998848 | tf_op jit(solution)/shard_map/all_to_all | solution.py:1006
  117.2 17.3 %rebuild.1 = (bf16[16,192,384]{2,1,0:T(8,128)(2,1)}, bf16[192,384]{1,0:T(8,128)(2,1)}, bf16[192,384]{1,0:T(8,128)(2,1)}, f32[48,48]{1,0:T(8,128)}) custom-call(bf16[8,1536,384]{2,1,0:T(8,128)(2,1)} %get-tuple-element.144.feat_ref, bf16[16,192,384]{2,1,0:T(8,128)(2,1)} %bitcast.57, bf16[16,192,384]{2,1,0:T(8,128)(2,1)} %bitcast.58, ...), custom_call_target="tpu_custom_call" | custom-call | flops 4831838208 | bytes 18874368 | tf_op jit(solution)/shard_map/rebuild/pallas_call | solution.py:899
  134.4 7.6 %all-to-all-done.1 = bf16[4,16,7808]{2,1,0:T(8,128)(2,1)S(1)} async-done(((bf16[4,16,7808]{2,1,0:T(8,128)(2,1)}), bf16[4,16,7808]{2,1,0:T(8,128)(2,1)S(1)}, u32[]{:S(2)}, u32[]{:S(2)}) %all-to-all-start.1) | async-done | bytes 999456 | tf_op jit(solution)/shard_map/all_to_all | solution.py:1006
  143.4 3.7 %all-to-all-start.2 = ((bf16[4,16,7808]{2,1,0:T(8,128)(2,1)}), bf16[4,16,7808]{2,1,0:T(8,128)(2,1)S(1)}, u32[]{:S(2)}, u32[]{:S(2)}) async-start(bf16[4,16,7808]{2,1,0:T(8,128)(2,1)} %broadcast_in_dim.18), calls=%async_computation.2 | async-start | bytes 1998848 | tf_op jit(solution)/shard_map/all_to_all | solution.py:1027
  147.2 21.0 %encode_backward.1 = (f32[16,192,384]{2,1,0:T(8,128)}, bf16[192,384]{1,0:T(8,128)(2,1)}, bf16[192,384]{1,0:T(8,128)(2,1)}, f32[48,48]{1,0:T(8,128)}) custom-call(bf16[8,1536,384]{2,1,0:T(8,128)(2,1)} %get-tuple-element.152.back_ref, bf16[16,192,384]{2,1,0:T(8,128)(2,1)} %bitcast.70, bf16[16,192,384]{2,1,0:T(8,128)(2,1)} %bitcast.71, ...), custom_call_target="tpu_custom_call" | custom-call | flops 4831838208 | bytes 18874368 | tf_op jit(solution)/shard_map/encode_backward/pallas_call | solution.py:899
  168.2 2.9 %all-to-all-done.2.refs_0_ = bf16[4,16,7808]{2,1,0:T(8,128)(2,1)S(1)} async-done(((bf16[4,16,7808]{2,1,0:T(8,128)(2,1)}), bf16[4,16,7808]{2,1,0:T(8,128)(2,1)S(1)}, u32[]{:S(2)}, u32[]{:S(2)}) %all-to-all-start.2) | async-done | bytes 999456 | tf_op jit(solution)/shard_map/all_to_all | solution.py:1027
  173.9 3.5 %all-to-all-start.3 = ((bf16[4,16,3072]{2,1,0:T(8,128)(2,1)}), bf16[4,16,3072]{2,1,0:T(8,128)(2,1)S(1)}, u32[]{:S(2)}, u32[]{:S(2)}) async-start(bf16[4,16,3072]{2,1,0:T(8,128)(2,1)} %broadcast_in_dim.19), calls=%async_computation.3 | async-start | bytes 786432 | tf_op jit(solution)/shard_map/all_to_all | solution.py:1027
  178.2 2.9 %collective-permute-start.11 = (f32[48,96]{1,0:T(8,128)S(1)}, f32[48,96]{1,0:T(8,128)S(1)}, u32[]{:S(2)}, u32[]{:S(2)}) collective-permute-start(f32[48,96]{1,0:T(8,128)S(1)} %pad_maximum_fusion.6), channel_id=1, source_target_pairs={{0,4},{1,5},{2,6},{3,7},{4,0},{5,1},{6,2},{7,3},{8,12},{9,13},{10,... | collective-permute-start | bytes 55304 | tf_op jit(solution)/shard_map/ppermute | solution.py:1021
  181.0 9.9 %collective-permute-done.11 = f32[48,96]{1,0:T(8,128)S(1)} collective-permute-done((f32[48,96]{1,0:T(8,128)S(1)}, f32[48,96]{1,0:T(8,128)S(1)}, u32[]{:S(2)}, u32[]{:S(2)}) %collective-permute-start.11) | collective-permute-done | bytes 18464 | tf_op jit(solution)/shard_map/ppermute | solution.py:1021
  191.8 3.8 %collective-permute-done.12 = f32[48,96]{1,0:T(8,128)S(1)} collective-permute-done((f32[48,96]{1,0:T(8,128)S(1)}, f32[48,96]{1,0:T(8,128)S(1)}, u32[]{:S(2)}, u32[]{:S(2)}) %collective-permute-start.12) | collective-permute-done | bytes 18464 | tf_op jit(solution)/shard_map/ppermute | solution.py:1021
  204.8 7.5 %finish.2 = (f32[32,16,1024]{2,1,0:T(8,128)}, f32[8,16,512]{2,1,0:T(8,128)}, f32[32,16,2048]{2,1,0:T(8,128)}, f32[32,16,1536]{2,1,0:T(8,128)}, f32[32,16,512]{2,...) custom-call(s32[5]{0:T(128)} %copy-done, bf16[4,16,7808]{2,1,0:T(8,128)(2,1)} %copy-done.3, ...), custom_call_target="tpu_custom_call" | custom-call | bytes 14991360 | tf_op jit(solution)/shard_map/finish/pallas_call | solution.py:1101
  214.5 2.5 %collective-permute-start.18 = (bf16[2,192,384]{2,1,0:T(8,128)(2,1)S(1)}, bf16[2,192,384]{2,1,0:T(8,128)(2,1)S(1)}, u32[]{:S(2)}, u32[]{:S(2)}) collective-permute-start(bf16[2,192,384]{2,1,0:T(8,128)(2,1)S(1)} %pad_maximum_fusion.2), channel_id=1, source_target_pairs={{0,8},{8,16},{16,24},{1,9},{9,17},{17,25},{2,10},{10,18},{18,26},{... | collective-permute-start | bytes 884744 | tf_op jit(solution)/shard_map/ppermute | solution.py:976
  218.4 3.7 %collective-permute-start.22 = (f32[48,96]{1,0:T(8,128)S(1)}, f32[48,96]{1,0:T(8,128)S(1)}, u32[]{:S(2)}, u32[]{:S(2)}) collective-permute-start(f32[48,96]{1,0:T(8,128)S(1)} %add.40), channel_id=1, source_target_pairs={{0,16},{8,24},{16,0},{24,8},{1,17},{9,25},{17,1},{25,9},{2,18},{10... | collective-permute-start | bytes 55304 | tf_op jit(solution)/shard_map/ppermute | solution.py:1254
  222.6 1.8 collective-permute-done.22
  226.2 5.2 %finish.3 = (f32[32,16,1024]{2,1,0:T(8,128)}, f32[8,16,512]{2,1,0:T(8,128)}, f32[32,16,2048]{2,1,0:T(8,128)}, f32[32,16,1536]{2,1,0:T(8,128)}, f32[32,16,512]{2,...) custom-call(s32[5]{0:T(128)} %copy-done, ...), custom_call_target="tpu_custom_call", output_to_operand_aliasing={{0}: (3, {}), {2}: (4, {}), {3}: (5, {}), {4}: (6, {}), {5}... | custom-call | bytes 4997120 | tf_op jit(solution)/shard_map/finish/pallas_call | solution.py:1101
  233.7 2.2 with_rims.1
  (116 shorter events, 39.1 us)
Async XLA Ops:
  1.9 17.0 %collective-permute-start = (bf16[2,192,384]{2,1,0:T(8,128)(2,1)S(1)}, bf16[2,192,384]{2,1,0:T(8,128)(2,1)S(1)}, u32[]{:S(2)}, u32[]{:S(2)}) collective-permute-start(bf16[2,192,384]{2,1,0:T(8,128)(2,1)S(1)} %pad_maximum_fusion), channel_id=1, source_target_pairs={{0,8},{8,16},{16,24},{1,9},{9,17},{17,25},{2,10},{10,18},{18,26},{... | collective-permute-start | bytes 884744 | tf_op jit(solution)/shard_map/ppermute | solution.py:976
  6.8 14.5 %collective-permute-start.1 = (bf16[2,192,384]{2,1,0:T(8,128)(2,1)S(1)}, bf16[2,192,384]{2,1,0:T(8,128)(2,1)S(1)}, u32[]{:S(2)}, u32[]{:S(2)}) collective-permute-start(bf16[2,192,384]{2,1,0:T(8,128)(2,1)S(1)} %pad_maximum_fusion.1), channel_id=1, source_target_pairs={{8,0},{16,8},{24,16},{9,1},{17,9},{25,17},{10,2},{18,10},{26,18},{... | collective-permute-start | bytes 884744 | tf_op jit(solution)/shard_map/ppermute | solution.py:976
  27.1 8.0 %collective-permute-start.2 = (bf16[384,512]{1,0:T(8,128)(2,1)}, bf16[384,512]{1,0:T(8,128)(2,1)S(1)}, u32[]{:S(2)}, u32[]{:S(2)}) collective-permute-start(bf16[384,512]{1,0:T(8,128)(2,1)} %get-tuple-element.114), channel_id=1, source_target_pairs={{0,8},{1,17},{2,10},{3,19},{4,12},{5,21},{6,14},{7,23},{8,0},{9,25... | collective-permute-start | bytes 1179656 | tf_op jit(solution)/shard_map/ppermute | solution.py:991
  35.2 7.8 %collective-permute-start.3 = (bf16[384,512]{1,0:T(8,128)(2,1)S(1)}, bf16[384,512]{1,0:T(8,128)(2,1)S(1)}, u32[]{:S(2)}, u32[]{:S(2)}) collective-permute-start(bf16[384,512]{1,0:T(8,128)(2,1)S(1)} %add_convert_fusion.3.part_ref.embed_part_ref), channel_id=1, source_target_pairs={{0,16},{1,9},{2,18},{3,11},{4,20},{5,13},{6,22},{7,15},{8,24},{9,1... | collective-permute-start | bytes 1179656 | tf_op jit(solution)/shard_map/ppermute | solution.py:991
  70.5 8.1 %collective-permute-start.4 = (bf16[384,512]{1,0:T(8,128)(2,1)}, bf16[384,512]{1,0:T(8,128)(2,1)S(1)}, u32[]{:S(2)}, u32[]{:S(2)}) collective-permute-start(bf16[384,512]{1,0:T(8,128)(2,1)} %get-tuple-element.123), channel_id=1, source_target_pairs={{0,8},{1,17},{2,10},{3,19},{4,12},{5,21},{6,14},{7,23},{8,0},{9,25... | collective-permute-start | bytes 1179656 | tf_op jit(solution)/shard_map/ppermute | solution.py:991
  78.5 1.9 collective-permute-start.6
  78.6 7.8 %collective-permute-start.5 = (bf16[384,512]{1,0:T(8,128)(2,1)S(1)}, bf16[384,512]{1,0:T(8,128)(2,1)S(1)}, u32[]{:S(2)}, u32[]{:S(2)}) collective-permute-start(bf16[384,512]{1,0:T(8,128)(2,1)S(1)} %add_convert_fusion.2.part_ref), channel_id=1, source_target_pairs={{0,16},{1,9},{2,18},{3,11},{4,20},{5,13},{6,22},{7,15},{8,24},{9,1... | collective-permute-start | bytes 1179656 | tf_op jit(solution)/shard_map/ppermute | solution.py:991
  86.5 20.3 %all-to-all-start = ((bf16[4,16,3072]{2,1,0:T(8,128)(2,1)}), bf16[4,16,3072]{2,1,0:T(8,128)(2,1)S(1)}, u32[]{:S(2)}, u32[]{:S(2)}) async-start(bf16[4,16,3072]{2,1,0:T(8,128)(2,1)} %bitcast.11), calls=%async_computation | async-start | bytes 786432 | tf_op jit(solution)/shard_map/all_to_all | solution.py:1006
  106.8 2.9 %collective-permute-start.7 = (bf16[64,7808]{1,0:T(8,128)(2,1)}, bf16[64,7808]{1,0:T(8,128)(2,1)S(1)}, u32[]{:S(2)}, u32[]{:S(2)}) collective-permute-start(bf16[64,7808]{1,0:T(8,128)(2,1)} %get-tuple-element.143), channel_id=1, source_target_pairs={{0,1},{1,0},{2,3},{3,2},{4,5},{5,4},{6,7},{7,6},{8,9},{9,8},{10,11... | collective-permute-start | bytes 2998280 | tf_op jit(solution)/shard_map/ppermute | solution.py:1021
  112.0 30.0 %all-to-all-start.1 = ((bf16[4,16,7808]{2,1,0:T(8,128)(2,1)}), bf16[4,16,7808]{2,1,0:T(8,128)(2,1)S(1)}, u32[]{:S(2)}, u32[]{:S(2)}) async-start(bf16[4,16,7808]{2,1,0:T(8,128)(2,1)} %bitcast.12), calls=%async_computation.1 | async-start | bytes 1998848 | tf_op jit(solution)/shard_map/all_to_all | solution.py:1006
  143.4 27.7 %all-to-all-start.2 = ((bf16[4,16,7808]{2,1,0:T(8,128)(2,1)}), bf16[4,16,7808]{2,1,0:T(8,128)(2,1)S(1)}, u32[]{:S(2)}, u32[]{:S(2)}) async-start(bf16[4,16,7808]{2,1,0:T(8,128)(2,1)} %broadcast_in_dim.18), calls=%async_computation.2 | async-start | bytes 1998848 | tf_op jit(solution)/shard_map/all_to_all | solution.py:1027
  147.1 30.2 %copy-start.17 = (f32[48,48]{1,0:T(8,128)S(1)}, f32[48,48]{1,0:T(8,128)}, u32[]{:S(2)}) copy-start(f32[48,48]{1,0:T(8,128)} %get-tuple-element.160) | copy-start | bytes 27652
  147.1 52.4 %copy-start.15 = (bf16[192,384]{1,0:T(8,128)(2,1)S(1)}, bf16[192,384]{1,0:T(8,128)(2,1)}, u32[]{:S(2)}) copy-start(bf16[192,384]{1,0:T(8,128)(2,1)} %get-tuple-element.163) | copy-start | bytes 442372
  168.1 32.3 %copy-start.14 = (bf16[192,384]{1,0:T(8,128)(2,1)S(1)}, bf16[192,384]{1,0:T(8,128)(2,1)}, u32[]{:S(2)}) copy-start(bf16[192,384]{1,0:T(8,128)(2,1)} %get-tuple-element.165) | copy-start | bytes 442372
  168.2 32.3 %copy-start.16 = (bf16[192,384]{1,0:T(8,128)(2,1)S(1)}, bf16[192,384]{1,0:T(8,128)(2,1)}, u32[]{:S(2)}) copy-start(bf16[192,384]{1,0:T(8,128)(2,1)} %get-tuple-element.166) | copy-start | bytes 442372
  171.1 33.1 %copy-start.3 = (bf16[4,16,7808]{2,1,0:T(8,128)(2,1)}, bf16[4,16,7808]{2,1,0:T(8,128)(2,1)S(1)}, u32[]{:S(2)}) copy-start(bf16[4,16,7808]{2,1,0:T(8,128)(2,1)S(1)} %all-to-all-done.2.refs_0_) | copy-start | bytes 2998276
  171.1 25.7 %collective-permute-start.8 = (bf16[4,16,7808]{2,1,0:T(8,128)(2,1)S(1)}, bf16[4,16,7808]{2,1,0:T(8,128)(2,1)}, u32[]{:S(2)}, u32[]{:S(2)}) collective-permute-start(bf16[4,16,7808]{2,1,0:T(8,128)(2,1)S(1)} %all-to-all-done.2.refs_0_), channel_id=1, source_target_pairs={{0,8},{1,17},{2,10},{3,19},{4,12},{5,21},{6,14},{7,23},{8,0},{9,25... | collective-permute-start | bytes 2998280 | tf_op jit(solution)/shard_map/ppermute | solution.py:991
  172.6 24.2 %collective-permute-start.9 = (bf16[4,16,7808]{2,1,0:T(8,128)(2,1)S(1)}, bf16[4,16,7808]{2,1,0:T(8,128)(2,1)}, u32[]{:S(2)}, u32[]{:S(2)}) collective-permute-start(bf16[4,16,7808]{2,1,0:T(8,128)(2,1)S(1)} %all-to-all-done.2.refs_0_), channel_id=1, source_target_pairs={{0,16},{1,9},{2,18},{3,11},{4,20},{5,13},{6,22},{7,15},{8,24},{9,1... | collective-permute-start | bytes 2998280 | tf_op jit(solution)/shard_map/ppermute | solution.py:991
  173.1 23.8 %collective-permute-start.10 = (bf16[4,16,7808]{2,1,0:T(8,128)(2,1)S(1)}, bf16[4,16,7808]{2,1,0:T(8,128)(2,1)S(1)}, u32[]{:S(2)}, u32[]{:S(2)}) collective-permute-start(bf16[4,16,7808]{2,1,0:T(8,128)(2,1)S(1)} %all-to-all-done.2.refs_0_), channel_id=1, source_target_pairs={{0,1},{1,0},{2,3},{3,2},{4,5},{5,4},{6,7},{7,6},{8,9},{9,8},{10,11... | collective-permute-start | bytes 2998280 | tf_op jit(solution)/shard_map/ppermute | solution.py:1021
  173.9 23.0 %all-to-all-start.3 = ((bf16[4,16,3072]{2,1,0:T(8,128)(2,1)}), bf16[4,16,3072]{2,1,0:T(8,128)(2,1)S(1)}, u32[]{:S(2)}, u32[]{:S(2)}) async-start(bf16[4,16,3072]{2,1,0:T(8,128)(2,1)} %broadcast_in_dim.19), calls=%async_computation.3 | async-start | bytes 786432 | tf_op jit(solution)/shard_map/all_to_all | solution.py:1027
  178.2 12.8 %collective-permute-start.11 = (f32[48,96]{1,0:T(8,128)S(1)}, f32[48,96]{1,0:T(8,128)S(1)}, u32[]{:S(2)}, u32[]{:S(2)}) collective-permute-start(f32[48,96]{1,0:T(8,128)S(1)} %pad_maximum_fusion.6), channel_id=1, source_target_pairs={{0,4},{1,5},{2,6},{3,7},{4,0},{5,1},{6,2},{7,3},{8,12},{9,13},{10,... | collective-permute-start | bytes 55304 | tf_op jit(solution)/shard_map/ppermute | solution.py:1021
  191.8 3.8 %collective-permute-start.12 = (f32[48,96]{1,0:T(8,128)S(1)}, f32[48,96]{1,0:T(8,128)S(1)}, u32[]{:S(2)}, u32[]{:S(2)}) collective-permute-start(f32[48,96]{1,0:T(8,128)S(1)} %fusion.6), channel_id=1, source_target_pairs={{0,2},{1,3},{2,0},{3,1},{4,6},{5,7},{6,4},{7,5},{8,10},{9,11},{10,... | collective-permute-start | bytes 55304 | tf_op jit(solution)/shard_map/ppermute | solution.py:1021
  195.6 1.2 collective-permute-start.13
  196.9 7.3 %collective-permute-start.16 = (bf16[4,16,7808]{2,1,0:T(8,128)(2,1)}, bf16[4,16,7808]{2,1,0:T(8,128)(2,1)}, u32[]{:S(2)}, u32[]{:S(2)}) collective-permute-start(bf16[4,16,7808]{2,1,0:T(8,128)(2,1)} %collective-permute-done.9.refs_2_), channel_id=1, source_target_pairs={{0,1},{1,0},{2,3},{3,2},{4,5},{5,4},{6,7},{7,6},{8,9},{9,8},{10,11... | collective-permute-start | bytes 2998280 | tf_op jit(solution)/shard_map/ppermute | solution.py:1021
  197.1 7.1 %collective-permute-start.17 = (bf16[4,16,7808]{2,1,0:T(8,128)(2,1)}, bf16[4,16,7808]{2,1,0:T(8,128)(2,1)}, u32[]{:S(2)}, u32[]{:S(2)}) collective-permute-start(bf16[4,16,7808]{2,1,0:T(8,128)(2,1)} %collective-permute-done.8.refs_1_), channel_id=1, source_target_pairs={{0,1},{1,0},{2,3},{3,2},{4,5},{5,4},{6,7},{7,6},{8,9},{9,8},{10,11... | collective-permute-start | bytes 2998280 | tf_op jit(solution)/shard_map/ppermute | solution.py:1021
  197.8 15.1 %collective-permute-start.14 = (bf16[4,16,7808]{2,1,0:T(8,128)(2,1)}, bf16[4,16,7808]{2,1,0:T(8,128)(2,1)}, u32[]{:S(2)}, u32[]{:S(2)}) collective-permute-start(bf16[4,16,7808]{2,1,0:T(8,128)(2,1)} %collective-permute-done.8.refs_1_), channel_id=1, source_target_pairs={{0,16},{1,9},{2,18},{3,11},{4,20},{5,13},{6,22},{7,15},{8,24},{9,1... | collective-permute-start | bytes 2998280 | tf_op jit(solution)/shard_map/ppermute | solution.py:991
  199.4 2.1 collective-permute-start.15
  212.9 12.2 %collective-permute-start.20 = (bf16[4,16,7808]{2,1,0:T(8,128)(2,1)}, bf16[4,16,7808]{2,1,0:T(8,128)(2,1)S(1)}, u32[]{:S(2)}, u32[]{:S(2)}) collective-permute-start(bf16[4,16,7808]{2,1,0:T(8,128)(2,1)} %collective-permute-done.14.refs_0_), channel_id=1, source_target_pairs={{0,1},{1,0},{2,3},{3,2},{4,5},{5,4},{6,7},{7,6},{8,9},{9,8},{10,11... | collective-permute-start | bytes 2998280 | tf_op jit(solution)/shard_map/ppermute | solution.py:1021
  213.1 5.2 %collective-permute-start.21 = (f32[48,96]{1,0:T(8,128)S(1)}, f32[48,96]{1,0:T(8,128)S(1)}, u32[]{:S(2)}, u32[]{:S(2)}) collective-permute-start(f32[48,96]{1,0:T(8,128)S(1)} %add.39), channel_id=1, source_target_pairs={{0,8},{8,0},{16,24},{24,16},{1,9},{9,1},{17,25},{25,17},{2,10},{10... | collective-permute-start | bytes 55304 | tf_op jit(solution)/shard_map/ppermute | solution.py:1254
  214.5 18.4 %collective-permute-start.18 = (bf16[2,192,384]{2,1,0:T(8,128)(2,1)S(1)}, bf16[2,192,384]{2,1,0:T(8,128)(2,1)S(1)}, u32[]{:S(2)}, u32[]{:S(2)}) collective-permute-start(bf16[2,192,384]{2,1,0:T(8,128)(2,1)S(1)} %pad_maximum_fusion.2), channel_id=1, source_target_pairs={{0,8},{8,16},{16,24},{1,9},{9,17},{17,25},{2,10},{10,18},{18,26},{... | collective-permute-start | bytes 884744 | tf_op jit(solution)/shard_map/ppermute | solution.py:976
  217.0 15.8 %collective-permute-start.19 = (bf16[2,192,384]{2,1,0:T(8,128)(2,1)S(1)}, bf16[2,192,384]{2,1,0:T(8,128)(2,1)S(1)}, u32[]{:S(2)}, u32[]{:S(2)}) collective-permute-start(bf16[2,192,384]{2,1,0:T(8,128)(2,1)S(1)} %pad_maximum_fusion.3), channel_id=1, source_target_pairs={{8,0},{16,8},{24,16},{9,1},{17,9},{25,17},{10,2},{18,10},{26,18},{... | collective-permute-start | bytes 884744 | tf_op jit(solution)/shard_map/ppermute | solution.py:976
  218.4 6.1 %collective-permute-start.22 = (f32[48,96]{1,0:T(8,128)S(1)}, f32[48,96]{1,0:T(8,128)S(1)}, u32[]{:S(2)}, u32[]{:S(2)}) collective-permute-start(f32[48,96]{1,0:T(8,128)S(1)} %add.40), channel_id=1, source_target_pairs={{0,16},{8,24},{16,0},{24,8},{1,17},{9,25},{17,1},{25,9},{2,18},{10... | collective-permute-start | bytes 55304 | tf_op jit(solution)/shard_map/ppermute | solution.py:1254
  (15 other events, 64.5 us)

commit v2 on v1

--- a/solution.py
+++ b/solution.py
@@ -1198,7 +1198,6 @@
     film_part = add(film_part, film_more)
     film_more = cross(film_part, 1)
     head_half_sum = add(head_own, swap_frames(head_other, 1))
-    film_more, head_half_sum = lax.optimization_barrier((film_more, head_half_sum))
     head_parts = split_over(head_half_sum, chip_groups())
     block_own, block_other, grad_profile = block_backward(
         columns, count, place, (film_part, film_more), embeds, stream, joined, attend, context, middle, active,
@@ -1250,8 +1249,8 @@
     )
     both_other = swap_frames(both, 1)
     rims_above, rims_below = send_along(rims[0], "rows", 1), send_along(rims[1], "rows", -1)
-    for distance in (1, 2):
-        covs = covs + lax.ppermute(covs, "rows", [(r, r ^ distance) for r in range(count)])
+    one, two, three = [lax.ppermute(covs, "rows", [(r, r ^ d) for r in range(count)]) for d in (1, 2, 3)]
+    covs = (covs + one) + (two + three)
     found = finish(slots_of, (3,), (both,), (both_other,), found, logits, model, hidden)
     prior_grad, misc, up_grad, qkv_grad, out_grad, down_grad = [
         array.reshape(-1, array.shape[-1]) for array in found[:6]

time: 237 us -> 234 us (0.987)
  waiting for transfers between devices: 40.7 us -> 38.1 us
    ppermute x7, waiting for transfers between devices: 6.83 us -> 2.66 us  [cross(): return lax.ppermute(values, ('rows', 'frames'), pairs)]
    ppermute x4, waiting for transfers between devices: 2.32 us -> 5.74 us  [send_along(): return lax.ppermute(values, axis, pairs)]
    ppermute x2 -> x3, starting transfers between devices: 5.06 us -> 3.49 us  [on_device(): lax.ppermute(covs, 'rows', [(r, r ^ d) for r in range(count)])]
  transfers between devices with their start and end apart: 27 -> 28, of which waited for: 14 -> 13; matrix products, arithmetic and copies ran while one was open for 6% -> 6% of each run, Pallas kernels for 39% -> 40%
where the time goes in v2:
time: 234 us; the launch traced here: 233 us
  Pallas kernels  126 us (54%)
  starting transfers between devices  44.5 us (19%)
  waiting for transfers between devices  38.1 us (16%)
  local copies, waits for them, and re-layouts  14.9 us (6%)
  other arithmetic  8.15 us (3%)
    pallas_call x2, Pallas kernels, scatter_call(): pl.pallas_call(kernel, grid=(steps + 1,), in_specs=[pl.BlockSpec((2, line...  38.2 us
    ppermute x10, waiting for transfers between devices, swap_frames(): lax.ppermute(values, 'frames', [(f, f ^ distance) for f in range(count)])  19.2 us
    pallas_call x1, Pallas kernels, decode(): pl.pallas_call(decode_kernel, grid=(map_rows // 2,), in_specs=[map_spec,...  16.9 us
    pallas_call x1, Pallas kernels, block_backward(): pl.pallas_call(functools.partial(block_backward_kernel, columns), in_spec...  15.4 us
    pallas_call x2, Pallas kernels, finish(): pl.pallas_call(functools.partial(finish_kernel, slots, widths), grid_spec...  12.6 us
    ppermute x4, starting transfers between devices, send_along(): return lax.ppermute(values, axis, pairs)  10.8 us
    pallas_call x2, Pallas kernels, decoded_grad(): pl.pallas_call(functools.partial(decoded_grad_kernel, base, map_rows // 2...  9.98 us
    all_to_all x2, starting transfers between devices, split_over(): return lax.all_to_all(split, 'frames', 0, 0, axis_index_groups=groups)  9.98 us
  transfers between devices with their start and end apart: 28, of which 13 were waited for; matrix products, arithmetic and copies ran while one was open for 6% of the time, Pallas kernels for 40%

profile of v2, /device:TPU:0, one launch (start us, length us, event | category | flops | bytes accessed | tf_op | source)
XLA Modules:
  0.0 233.2 jit_solution(12532836176783498193)
XLA Ops:
  1.9 4.9 %collective-permute-start = (bf16[2,192,384]{2,1,0:T(8,128)(2,1)S(1)}, bf16[2,192,384]{2,1,0:T(8,128)(2,1)S(1)}, u32[]{:S(2)}, u32[]{:S(2)}) collective-permute-start(bf16[2,192,384]{2,1,0:T(8,128)(2,1)S(1)} %pad_maximum_fusion), channel_id=1, source_target_pairs={{0,8},{8,16},{16,24},{1,9},{9,17},{17,25},{2,10},{10,18},{18,26},{... | collective-permute-start | bytes 884744 | tf_op jit(solution)/shard_map/ppermute | solution.py:976
  8.1 2.1 expand.1
  10.2 8.7 %encode_inner.1 = (bf16[8,1536,384]{2,1,0:T(8,128)(2,1)}, bf16[288,384]{1,0:T(8,128)(2,1)}) custom-call(bf16[16,192,384]{2,1,0:T(8,128)(2,1)} %bitcast.63, bf16[16,192,384]{2,1,0:T(8,128)(2,1)} %bitcast.64, bf16[16,192,384]{2,1,0:T(8,128)(2,1)} %bitcast.65, bf16[16,192,384]{2,1,0:T(8,128)(2,1)} %bitcast.66, ...), custom_call_target="tpu_custom_call" | custom-call | flops 1811939328 | bytes 14155776 | tf_op jit(solution)/shard_map/encode_inner/pallas_call | solution.py:286
  18.9 2.3 collective-permute-done.1.down_ref
  22.0 5.1 %encode_edge.1 = (bf16[8,1536,384]{2,1,0:T(8,128)(2,1)}, bf16[384,384]{1,0:T(8,128)(2,1)}, bf16[384,512]{1,0:T(8,128)(2,1)}) custom-call(bf16[16,192,384]{2,1,0:T(8,128)(2,1)} %bitcast.67, bf16[16,192,384]{2,1,0:T(8,128)(2,1)} %bitcast.68, bf16[16,192,384]{2,1,0:T(8,128)(2,1)} %bitcast.69, ...), custom_call_target="tpu_custom_call", output_to_operand_aliasing={{0}: (8, {})} | custom-call | flops 603979776 | bytes 4718592 | tf_op jit(solution)/shard_map/encode_edge/pallas_call | solution.py:323
  29.3 5.0 %decoded_grad.2.rest_0_ = bf16[8,1536,384]{2,1,0:T(8,128)(2,1)} custom-call(bf16[16,192,384]{2,1,0:T(8,128)(2,1)} %bitcast.46, bf16[16,192,384]{2,1,0:T(8,128)(2,1)} %bitcast.47, bf16[16,192,384]{2,1,0:T(8,128)(2,1)} %bitcast.48, bf16[16,192,384]{2,1,0:T(8,128)(2,1)} %bitcast.49, bf16[2,192,384]{2,1,0:T(8,128)(2,1)} %copy-done.2, ...), custom_call_target="tpu_custom_call" | custom-call | flops 1207959552 | bytes 4718592 | tf_op jit(solution)/shard_map/decoded_grad/pallas_call | solution.py:500
  37.2 5.0 %decoded_grad.3.grad_ref = bf16[8,1536,384]{2,1,0:T(8,128)(2,1)} custom-call(bf16[16,192,384]{2,1,0:T(8,128)(2,1)} %bitcast.51, bf16[16,192,384]{2,1,0:T(8,128)(2,1)} %bitcast.52, bf16[16,192,384]{2,1,0:T(8,128)(2,1)} %bitcast.53, bf16[16,192,384]{2,1,0:T(8,128)(2,1)} %bitcast.54, bf16[16,192,384]{2,1,0:T(8,128)(2,1)} %bitcast.55, ...), custom_call_target="tpu_custom_call", output_to_operand_aliasing={{}: (9, {})} | custom-call | flops 1207959552 | bytes 4718592 | tf_op jit(solution)/shard_map/decoded_grad/pallas_call | solution.py:500
  43.8 9.7 %block_forward.1 = (bf16[384,1536]{1,0:T(8,128)(2,1)}, bf16[12,128,256]{2,1,0:T(8,128)(2,1)}, bf16[384,512]{1,0:T(8,128)(2,1)}, f32[384,512]{1,0:T(8,128)}, bf16...) custom-call(bf16[384,512]{1,0:T(8,128)(2,1)} %copy-done.4, ...), custom_call_target="tpu_custom_call" | custom-call | flops 2415919104 | bytes 16777216 | tf_op jit(solution)/shard_map/block_forward/pallas_call | solution.py:461
  53.6 16.9 %decode.1 = (bf16[8,1536,384]{2,1,0:T(8,128)(2,1)}, bf16[48,384]{1,0:T(8,128)(2,1)}, bf16[384,384]{1,0:T(8,128)(2,1)}, bf16[384,512]{1,0:T(8,128)(2,1)}) custom-call(bf16[8,1536,384]{2,1,0:T(8,128)(2,1)} %get-tuple-element.140.feat_ref, bf16[8,1536,384]{2,1,0:T(8,128)(2,1)} %decoded_grad.3.grad_ref, f32[48,384]{1,0:T(8,128)} %get-tuple-element.119.scale_ref, ...), custom_call_target="tpu_custom_call" | custom-call | flops 94371840 | bytes 28311552 | tf_op jit(solution)/shard_map/decode/pallas_call | solution.py:576
  73.4 4.0 %heads.1 = (bf16[64,3072]{1,0:T(8,128)(2,1)}, bf16[64,3072]{1,0:T(8,128)(2,1)}, f32[384,512]{1,0:T(8,128)}) custom-call(s32[2]{0:T(128)} %pad_add_fusion.place_ref, bf16[384,512]{1,0:T(8,128)(2,1)} %get-tuple-element.122.state_ref, bf16[384,1024]{1,0:T(8,128)(2,1)} %cot_ref.1, f32[384,128]{1,0:T(8,128)} %broadcast_in_dim.17.live_ref, ...), custom_call_target="tpu_custom_call" | custom-call | flops 805306368 | bytes 4194304 | tf_op jit(solution)/shard_map/heads/pallas_call | solution.py:637
  80.5 1.8 add_convert_fusion.1
  82.3 4.9 %all-to-all-start = ((bf16[4,16,3072]{2,1,0:T(8,128)(2,1)}), bf16[4,16,3072]{2,1,0:T(8,128)(2,1)S(1)}, u32[]{:S(2)}, u32[]{:S(2)}) async-start(bf16[4,16,3072]{2,1,0:T(8,128)(2,1)} %bitcast.11), calls=%async_computation | async-start | bytes 786432 | tf_op jit(solution)/shard_map/all_to_all | solution.py:1006
  87.9 15.4 %block_backward.1 = (bf16[64,7808]{1,0:T(8,128)(2,1)}, bf16[64,7808]{1,0:T(8,128)(2,1)}, f32[384,384]{1,0:T(8,128)}) custom-call(s32[2]{0:T(128)} %pad_add_fusion.place_ref, bf16[384,512]{1,0:T(8,128)(2,1)} %copy-done.5, bf16[384,512]{1,0:T(8,128)(2,1)} %copy-done.11, bf16[384,512]{1,0:T(8,128)(2,1)} %copy-done.4, bf16[384,512]{1,0:T(8,128)(2,1)} %copy-done.10, ...), custom_call_target="tpu_custom_call" | custom-call | flops 3623878656 | bytes 20971520 | tf_op jit(solution)/shard_map/block_backward/pallas_call | solution.py:762
  103.4 2.8 %collective-permute-done.7 = bf16[64,7808]{1,0:T(8,128)(2,1)S(1)} collective-permute-done((bf16[64,7808]{1,0:T(8,128)(2,1)}, bf16[64,7808]{1,0:T(8,128)(2,1)S(1)}, u32[]{:S(2)}, u32[]{:S(2)}) %collective-permute-start.7) | collective-permute-done | bytes 999456 | tf_op jit(solution)/shard_map/ppermute | solution.py:1021
  106.2 2.4 %add_convert_fusion = bf16[64,7808]{1,0:T(8,128)(2,1)} fusion(bf16[64,7808]{1,0:T(8,128)(2,1)S(1)} %collective-permute-done.7, bf16[64,7808]{1,0:T(8,128)(2,1)} %get-tuple-element.135), kind=kLoop, calls=%fused_computation | loop fusion | flops 1998848 | bytes 2998272 | tf_op jit(solution)/shard_map/convert_element_type | solution.py:995
  108.6 5.1 %all-to-all-start.1 = ((bf16[4,16,7808]{2,1,0:T(8,128)(2,1)}), bf16[4,16,7808]{2,1,0:T(8,128)(2,1)S(1)}, u32[]{:S(2)}, u32[]{:S(2)}) async-start(bf16[4,16,7808]{2,1,0:T(8,128)(2,1)} %bitcast.12), calls=%async_computation.1 | async-start | bytes 1998848 | tf_op jit(solution)/shard_map/all_to_all | solution.py:1006
  113.8 17.3 %rebuild.1 = (bf16[16,192,384]{2,1,0:T(8,128)(2,1)}, bf16[192,384]{1,0:T(8,128)(2,1)}, bf16[192,384]{1,0:T(8,128)(2,1)}, f32[48,48]{1,0:T(8,128)}) custom-call(bf16[8,1536,384]{2,1,0:T(8,128)(2,1)} %get-tuple-element.140.feat_ref, bf16[16,192,384]{2,1,0:T(8,128)(2,1)} %bitcast.57, bf16[16,192,384]{2,1,0:T(8,128)(2,1)} %bitcast.58, ...), custom_call_target="tpu_custom_call" | custom-call | flops 4831838208 | bytes 18874368 | tf_op jit(solution)/shard_map/rebuild/pallas_call | solution.py:899
  131.0 7.6 %all-to-all-done.1 = bf16[4,16,7808]{2,1,0:T(8,128)(2,1)S(1)} async-done(((bf16[4,16,7808]{2,1,0:T(8,128)(2,1)}), bf16[4,16,7808]{2,1,0:T(8,128)(2,1)S(1)}, u32[]{:S(2)}, u32[]{:S(2)}) %all-to-all-start.1) | async-done | bytes 999456 | tf_op jit(solution)/shard_map/all_to_all | solution.py:1006
  140.0 3.7 %all-to-all-start.2 = ((bf16[4,16,7808]{2,1,0:T(8,128)(2,1)}), bf16[4,16,7808]{2,1,0:T(8,128)(2,1)S(1)}, u32[]{:S(2)}, u32[]{:S(2)}) async-start(bf16[4,16,7808]{2,1,0:T(8,128)(2,1)} %broadcast_in_dim.18), calls=%async_computation.2 | async-start | bytes 1998848 | tf_op jit(solution)/shard_map/all_to_all | solution.py:1027
  143.7 21.0 %encode_backward.1 = (f32[16,192,384]{2,1,0:T(8,128)}, bf16[192,384]{1,0:T(8,128)(2,1)}, bf16[192,384]{1,0:T(8,128)(2,1)}, f32[48,48]{1,0:T(8,128)}) custom-call(bf16[8,1536,384]{2,1,0:T(8,128)(2,1)} %get-tuple-element.148.back_ref, bf16[16,192,384]{2,1,0:T(8,128)(2,1)} %bitcast.70, bf16[16,192,384]{2,1,0:T(8,128)(2,1)} %bitcast.71, ...), custom_call_target="tpu_custom_call" | custom-call | flops 4831838208 | bytes 18874368 | tf_op jit(solution)/shard_map/encode_backward/pallas_call | solution.py:899
  164.7 2.9 %all-to-all-done.2.refs_0_ = bf16[4,16,7808]{2,1,0:T(8,128)(2,1)S(1)} async-done(((bf16[4,16,7808]{2,1,0:T(8,128)(2,1)}), bf16[4,16,7808]{2,1,0:T(8,128)(2,1)S(1)}, u32[]{:S(2)}, u32[]{:S(2)}) %all-to-all-start.2) | async-done | bytes 999456 | tf_op jit(solution)/shard_map/all_to_all | solution.py:1027
  170.4 3.5 %all-to-all-start.3 = ((bf16[4,16,3072]{2,1,0:T(8,128)(2,1)}), bf16[4,16,3072]{2,1,0:T(8,128)(2,1)S(1)}, u32[]{:S(2)}, u32[]{:S(2)}) async-start(bf16[4,16,3072]{2,1,0:T(8,128)(2,1)} %broadcast_in_dim.19), calls=%async_computation.3 | async-start | bytes 786432 | tf_op jit(solution)/shard_map/all_to_all | solution.py:1027
  174.7 2.9 %collective-permute-start.11 = (f32[48,96]{1,0:T(8,128)S(1)}, f32[48,96]{1,0:T(8,128)S(1)}, u32[]{:S(2)}, u32[]{:S(2)}) collective-permute-start(f32[48,96]{1,0:T(8,128)S(1)} %pad_maximum_fusion.6), channel_id=1, source_target_pairs={{0,4},{1,5},{2,6},{3,7},{4,0},{5,1},{6,2},{7,3},{8,12},{9,13},{10,... | collective-permute-start | bytes 55304 | tf_op jit(solution)/shard_map/ppermute | solution.py:1021
  177.6 9.9 %collective-permute-done.11 = f32[48,96]{1,0:T(8,128)S(1)} collective-permute-done((f32[48,96]{1,0:T(8,128)S(1)}, f32[48,96]{1,0:T(8,128)S(1)}, u32[]{:S(2)}, u32[]{:S(2)}) %collective-permute-start.11) | collective-permute-done | bytes 18464 | tf_op jit(solution)/shard_map/ppermute | solution.py:1021
  188.4 3.8 %collective-permute-done.12 = f32[48,96]{1,0:T(8,128)S(1)} collective-permute-done((f32[48,96]{1,0:T(8,128)S(1)}, f32[48,96]{1,0:T(8,128)S(1)}, u32[]{:S(2)}, u32[]{:S(2)}) %collective-permute-start.12) | collective-permute-done | bytes 18464 | tf_op jit(solution)/shard_map/ppermute | solution.py:1021
  194.4 1.6 collective-permute-start.14
  201.3 7.5 %finish.2 = (f32[32,16,1024]{2,1,0:T(8,128)}, f32[8,16,512]{2,1,0:T(8,128)}, f32[32,16,2048]{2,1,0:T(8,128)}, f32[32,16,1536]{2,1,0:T(8,128)}, f32[32,16,512]{2,...) custom-call(s32[5]{0:T(128)} %copy-done, bf16[4,16,7808]{2,1,0:T(8,128)(2,1)} %copy-done.3, ...), custom_call_target="tpu_custom_call" | custom-call | bytes 14991360 | tf_op jit(solution)/shard_map/finish/pallas_call | solution.py:1101
  210.6 2.0 collective-permute-start.23
  213.2 3.3 %collective-permute-start.18 = (bf16[2,192,384]{2,1,0:T(8,128)(2,1)S(1)}, bf16[2,192,384]{2,1,0:T(8,128)(2,1)S(1)}, u32[]{:S(2)}, u32[]{:S(2)}) collective-permute-start(bf16[2,192,384]{2,1,0:T(8,128)(2,1)S(1)} %pad_maximum_fusion.2), channel_id=1, source_target_pairs={{0,8},{8,16},{16,24},{1,9},{9,17},{17,25},{2,10},{10,18},{18,26},{... | collective-permute-start | bytes 884744 | tf_op jit(solution)/shard_map/ppermute | solution.py:976
  220.1 5.2 %finish.3 = (f32[32,16,1024]{2,1,0:T(8,128)}, f32[8,16,512]{2,1,0:T(8,128)}, f32[32,16,2048]{2,1,0:T(8,128)}, f32[32,16,1536]{2,1,0:T(8,128)}, f32[32,16,512]{2,...) custom-call(s32[5]{0:T(128)} %copy-done, ...), custom_call_target="tpu_custom_call", output_to_operand_aliasing={{0}: (3, {}), {2}: (4, {}), {3}: (5, {}), {4}: (6, {}), {5}... | custom-call | bytes 4997120 | tf_op jit(solution)/shard_map/finish/pallas_call | solution.py:1101
  226.9 3.4 %collective-permute-done.19.below_ref = bf16[2,192,384]{2,1,0:T(8,128)(2,1)S(1)} collective-permute-done((bf16[2,192,384]{2,1,0:T(8,128)(2,1)S(1)}, bf16[2,192,384]{2,1,0:T(8,128)(2,1)S(1)}, u32[]{:S(2)}, u32[]{:S(2)}) %collective-permute-start.19) | collective-permute-done | bytes 294944 | tf_op jit(solution)/shard_map/ppermute | solution.py:976
  231.0 2.2 with_rims.1
  (117 shorter events, 38.3 us)
Async XLA Ops:
  1.9 17.0 %collective-permute-start = (bf16[2,192,384]{2,1,0:T(8,128)(2,1)S(1)}, bf16[2,192,384]{2,1,0:T(8,128)(2,1)S(1)}, u32[]{:S(2)}, u32[]{:S(2)}) collective-permute-start(bf16[2,192,384]{2,1,0:T(8,128)(2,1)S(1)} %pad_maximum_fusion), channel_id=1, source_target_pairs={{0,8},{8,16},{16,24},{1,9},{9,17},{17,25},{2,10},{10,18},{18,26},{... | collective-permute-start | bytes 884744 | tf_op jit(solution)/shard_map/ppermute | solution.py:976
  6.8 14.5 %collective-permute-start.1 = (bf16[2,192,384]{2,1,0:T(8,128)(2,1)S(1)}, bf16[2,192,384]{2,1,0:T(8,128)(2,1)S(1)}, u32[]{:S(2)}, u32[]{:S(2)}) collective-permute-start(bf16[2,192,384]{2,1,0:T(8,128)(2,1)S(1)} %pad_maximum_fusion.1), channel_id=1, source_target_pairs={{8,0},{16,8},{24,16},{9,1},{17,9},{25,17},{10,2},{18,10},{26,18},{... | collective-permute-start | bytes 884744 | tf_op jit(solution)/shard_map/ppermute | solution.py:976
  27.1 8.0 %collective-permute-start.2 = (bf16[384,512]{1,0:T(8,128)(2,1)}, bf16[384,512]{1,0:T(8,128)(2,1)S(1)}, u32[]{:S(2)}, u32[]{:S(2)}) collective-permute-start(bf16[384,512]{1,0:T(8,128)(2,1)} %get-tuple-element.112), channel_id=1, source_target_pairs={{0,8},{1,17},{2,10},{3,19},{4,12},{5,21},{6,14},{7,23},{8,0},{9,25... | collective-permute-start | bytes 1179656 | tf_op jit(solution)/shard_map/ppermute | solution.py:991
  35.2 7.8 %collective-permute-start.3 = (bf16[384,512]{1,0:T(8,128)(2,1)S(1)}, bf16[384,512]{1,0:T(8,128)(2,1)S(1)}, u32[]{:S(2)}, u32[]{:S(2)}) collective-permute-start(bf16[384,512]{1,0:T(8,128)(2,1)S(1)} %add_convert_fusion.3.part_ref.embed_part_ref), channel_id=1, source_target_pairs={{0,16},{1,9},{2,18},{3,11},{4,20},{5,13},{6,22},{7,15},{8,24},{9,1... | collective-permute-start | bytes 1179656 | tf_op jit(solution)/shard_map/ppermute | solution.py:991
  70.5 8.1 %collective-permute-start.4 = (bf16[384,512]{1,0:T(8,128)(2,1)}, bf16[384,512]{1,0:T(8,128)(2,1)S(1)}, u32[]{:S(2)}, u32[]{:S(2)}) collective-permute-start(bf16[384,512]{1,0:T(8,128)(2,1)} %get-tuple-element.121), channel_id=1, source_target_pairs={{0,8},{1,17},{2,10},{3,19},{4,12},{5,21},{6,14},{7,23},{8,0},{9,25... | collective-permute-start | bytes 1179656 | tf_op jit(solution)/shard_map/ppermute | solution.py:991
  78.5 1.9 collective-permute-start.6
  78.6 8.5 %collective-permute-start.5 = (bf16[384,512]{1,0:T(8,128)(2,1)S(1)}, bf16[384,512]{1,0:T(8,128)(2,1)S(1)}, u32[]{:S(2)}, u32[]{:S(2)}) collective-permute-start(bf16[384,512]{1,0:T(8,128)(2,1)S(1)} %add_convert_fusion.2.part_ref), channel_id=1, source_target_pairs={{0,16},{1,9},{2,18},{3,11},{4,20},{5,13},{6,22},{7,15},{8,24},{9,1... | collective-permute-start | bytes 1179656 | tf_op jit(solution)/shard_map/ppermute | solution.py:991
  82.3 21.0 %all-to-all-start = ((bf16[4,16,3072]{2,1,0:T(8,128)(2,1)}), bf16[4,16,3072]{2,1,0:T(8,128)(2,1)S(1)}, u32[]{:S(2)}, u32[]{:S(2)}) async-start(bf16[4,16,3072]{2,1,0:T(8,128)(2,1)} %bitcast.11), calls=%async_computation | async-start | bytes 786432 | tf_op jit(solution)/shard_map/all_to_all | solution.py:1006
  103.3 2.9 %collective-permute-start.7 = (bf16[64,7808]{1,0:T(8,128)(2,1)}, bf16[64,7808]{1,0:T(8,128)(2,1)S(1)}, u32[]{:S(2)}, u32[]{:S(2)}) collective-permute-start(bf16[64,7808]{1,0:T(8,128)(2,1)} %get-tuple-element.139), channel_id=1, source_target_pairs={{0,1},{1,0},{2,3},{3,2},{4,5},{5,4},{6,7},{7,6},{8,9},{9,8},{10,11... | collective-permute-start | bytes 2998280 | tf_op jit(solution)/shard_map/ppermute | solution.py:1021
  108.6 30.1 %all-to-all-start.1 = ((bf16[4,16,7808]{2,1,0:T(8,128)(2,1)}), bf16[4,16,7808]{2,1,0:T(8,128)(2,1)S(1)}, u32[]{:S(2)}, u32[]{:S(2)}) async-start(bf16[4,16,7808]{2,1,0:T(8,128)(2,1)} %bitcast.12), calls=%async_computation.1 | async-start | bytes 1998848 | tf_op jit(solution)/shard_map/all_to_all | solution.py:1006
  140.0 27.7 %all-to-all-start.2 = ((bf16[4,16,7808]{2,1,0:T(8,128)(2,1)}), bf16[4,16,7808]{2,1,0:T(8,128)(2,1)S(1)}, u32[]{:S(2)}, u32[]{:S(2)}) async-start(bf16[4,16,7808]{2,1,0:T(8,128)(2,1)} %broadcast_in_dim.18), calls=%async_computation.2 | async-start | bytes 1998848 | tf_op jit(solution)/shard_map/all_to_all | solution.py:1027
  143.7 52.3 %copy-start.15 = (bf16[192,384]{1,0:T(8,128)(2,1)S(1)}, bf16[192,384]{1,0:T(8,128)(2,1)}, u32[]{:S(2)}) copy-start(bf16[192,384]{1,0:T(8,128)(2,1)} %get-tuple-element.159) | copy-start | bytes 442372
  164.7 32.3 %copy-start.14 = (bf16[192,384]{1,0:T(8,128)(2,1)S(1)}, bf16[192,384]{1,0:T(8,128)(2,1)}, u32[]{:S(2)}) copy-start(bf16[192,384]{1,0:T(8,128)(2,1)} %get-tuple-element.161) | copy-start | bytes 442372
  164.7 32.3 %copy-start.16 = (bf16[192,384]{1,0:T(8,128)(2,1)S(1)}, bf16[192,384]{1,0:T(8,128)(2,1)}, u32[]{:S(2)}) copy-start(bf16[192,384]{1,0:T(8,128)(2,1)} %get-tuple-element.162) | copy-start | bytes 442372
  167.7 33.1 %copy-start.3 = (bf16[4,16,7808]{2,1,0:T(8,128)(2,1)}, bf16[4,16,7808]{2,1,0:T(8,128)(2,1)S(1)}, u32[]{:S(2)}) copy-start(bf16[4,16,7808]{2,1,0:T(8,128)(2,1)S(1)} %all-to-all-done.2.refs_0_) | copy-start | bytes 2998276
  167.7 25.7 %collective-permute-start.8 = (bf16[4,16,7808]{2,1,0:T(8,128)(2,1)S(1)}, bf16[4,16,7808]{2,1,0:T(8,128)(2,1)}, u32[]{:S(2)}, u32[]{:S(2)}) collective-permute-start(bf16[4,16,7808]{2,1,0:T(8,128)(2,1)S(1)} %all-to-all-done.2.refs_0_), channel_id=1, source_target_pairs={{0,8},{1,17},{2,10},{3,19},{4,12},{5,21},{6,14},{7,23},{8,0},{9,25... | collective-permute-start | bytes 2998280 | tf_op jit(solution)/shard_map/ppermute | solution.py:991
  169.2 24.2 %collective-permute-start.9 = (bf16[4,16,7808]{2,1,0:T(8,128)(2,1)S(1)}, bf16[4,16,7808]{2,1,0:T(8,128)(2,1)}, u32[]{:S(2)}, u32[]{:S(2)}) collective-permute-start(bf16[4,16,7808]{2,1,0:T(8,128)(2,1)S(1)} %all-to-all-done.2.refs_0_), channel_id=1, source_target_pairs={{0,16},{1,9},{2,18},{3,11},{4,20},{5,13},{6,22},{7,15},{8,24},{9,1... | collective-permute-start | bytes 2998280 | tf_op jit(solution)/shard_map/ppermute | solution.py:991
  169.6 23.8 %collective-permute-start.10 = (bf16[4,16,7808]{2,1,0:T(8,128)(2,1)S(1)}, bf16[4,16,7808]{2,1,0:T(8,128)(2,1)S(1)}, u32[]{:S(2)}, u32[]{:S(2)}) collective-permute-start(bf16[4,16,7808]{2,1,0:T(8,128)(2,1)S(1)} %all-to-all-done.2.refs_0_), channel_id=1, source_target_pairs={{0,1},{1,0},{2,3},{3,2},{4,5},{5,4},{6,7},{7,6},{8,9},{9,8},{10,11... | collective-permute-start | bytes 2998280 | tf_op jit(solution)/shard_map/ppermute | solution.py:1021
  170.4 23.0 %all-to-all-start.3 = ((bf16[4,16,3072]{2,1,0:T(8,128)(2,1)}), bf16[4,16,3072]{2,1,0:T(8,128)(2,1)S(1)}, u32[]{:S(2)}, u32[]{:S(2)}) async-start(bf16[4,16,3072]{2,1,0:T(8,128)(2,1)} %broadcast_in_dim.19), calls=%async_computation.3 | async-start | bytes 786432 | tf_op jit(solution)/shard_map/all_to_all | solution.py:1027
  174.7 12.8 %collective-permute-start.11 = (f32[48,96]{1,0:T(8,128)S(1)}, f32[48,96]{1,0:T(8,128)S(1)}, u32[]{:S(2)}, u32[]{:S(2)}) collective-permute-start(f32[48,96]{1,0:T(8,128)S(1)} %pad_maximum_fusion.6), channel_id=1, source_target_pairs={{0,4},{1,5},{2,6},{3,7},{4,0},{5,1},{6,2},{7,3},{8,12},{9,13},{10,... | collective-permute-start | bytes 55304 | tf_op jit(solution)/shard_map/ppermute | solution.py:1021
  188.4 3.8 %collective-permute-start.12 = (f32[48,96]{1,0:T(8,128)S(1)}, f32[48,96]{1,0:T(8,128)S(1)}, u32[]{:S(2)}, u32[]{:S(2)}) collective-permute-start(f32[48,96]{1,0:T(8,128)S(1)} %fusion.6), channel_id=1, source_target_pairs={{0,2},{1,3},{2,0},{3,1},{4,6},{5,7},{6,4},{7,5},{8,10},{9,11},{10,... | collective-permute-start | bytes 55304 | tf_op jit(solution)/shard_map/ppermute | solution.py:1021
  192.2 1.2 collective-permute-start.13
  193.4 7.3 %collective-permute-start.16 = (bf16[4,16,7808]{2,1,0:T(8,128)(2,1)}, bf16[4,16,7808]{2,1,0:T(8,128)(2,1)}, u32[]{:S(2)}, u32[]{:S(2)}) collective-permute-start(bf16[4,16,7808]{2,1,0:T(8,128)(2,1)} %collective-permute-done.9.refs_2_), channel_id=1, source_target_pairs={{0,1},{1,0},{2,3},{3,2},{4,5},{5,4},{6,7},{7,6},{8,9},{9,8},{10,11... | collective-permute-start | bytes 2998280 | tf_op jit(solution)/shard_map/ppermute | solution.py:1021
  193.7 7.1 %collective-permute-start.17 = (bf16[4,16,7808]{2,1,0:T(8,128)(2,1)}, bf16[4,16,7808]{2,1,0:T(8,128)(2,1)}, u32[]{:S(2)}, u32[]{:S(2)}) collective-permute-start(bf16[4,16,7808]{2,1,0:T(8,128)(2,1)} %collective-permute-done.8.refs_1_), channel_id=1, source_target_pairs={{0,1},{1,0},{2,3},{3,2},{4,5},{5,4},{6,7},{7,6},{8,9},{9,8},{10,11... | collective-permute-start | bytes 2998280 | tf_op jit(solution)/shard_map/ppermute | solution.py:1021
  194.4 15.1 %collective-permute-start.14 = (bf16[4,16,7808]{2,1,0:T(8,128)(2,1)}, bf16[4,16,7808]{2,1,0:T(8,128)(2,1)}, u32[]{:S(2)}, u32[]{:S(2)}) collective-permute-start(bf16[4,16,7808]{2,1,0:T(8,128)(2,1)} %collective-permute-done.8.refs_1_), channel_id=1, source_target_pairs={{0,16},{1,9},{2,18},{3,11},{4,20},{5,13},{6,22},{7,15},{8,24},{9,1... | collective-permute-start | bytes 2998280 | tf_op jit(solution)/shard_map/ppermute | solution.py:991
  196.0 2.1 collective-permute-start.15
  209.5 9.6 %collective-permute-start.20 = (bf16[4,16,7808]{2,1,0:T(8,128)(2,1)}, bf16[4,16,7808]{2,1,0:T(8,128)(2,1)S(1)}, u32[]{:S(2)}, u32[]{:S(2)}) collective-permute-start(bf16[4,16,7808]{2,1,0:T(8,128)(2,1)} %collective-permute-done.14.refs_0_), channel_id=1, source_target_pairs={{0,1},{1,0},{2,3},{3,2},{4,5},{5,4},{6,7},{7,6},{8,9},{9,8},{10,11... | collective-permute-start | bytes 2998280 | tf_op jit(solution)/shard_map/ppermute | solution.py:1021
  209.7 7.4 %collective-permute-start.22 = (f32[48,96]{1,0:T(8,128)S(1)}, f32[48,96]{1,0:T(8,128)S(1)}, u32[]{:S(2)}, u32[]{:S(2)}) collective-permute-start(f32[48,96]{1,0:T(8,128)S(1)} %add.42), channel_id=1, source_target_pairs={{0,16},{8,24},{16,0},{24,8},{1,17},{9,25},{17,1},{25,9},{2,18},{10... | collective-permute-start | bytes 55304 | tf_op jit(solution)/shard_map/ppermute | solution.py:1252
  210.6 7.8 %collective-permute-start.23 = (f32[48,96]{1,0:T(8,128)S(1)}, f32[48,96]{1,0:T(8,128)S(1)}, u32[]{:S(2)}, u32[]{:S(2)}) collective-permute-start(f32[48,96]{1,0:T(8,128)S(1)} %add.42), channel_id=1, source_target_pairs={{0,24},{8,16},{16,8},{24,0},{1,25},{9,17},{17,9},{25,1},{2,26},{10... | collective-permute-start | bytes 55304 | tf_op jit(solution)/shard_map/ppermute | solution.py:1252
  212.6 5.8 %collective-permute-start.21 = (f32[48,96]{1,0:T(8,128)S(1)}, f32[48,96]{1,0:T(8,128)S(1)}, u32[]{:S(2)}, u32[]{:S(2)}) collective-permute-start(f32[48,96]{1,0:T(8,128)S(1)} %add.42), channel_id=1, source_target_pairs={{0,8},{8,0},{16,24},{24,16},{1,9},{9,1},{17,25},{25,17},{2,10},{10... | collective-permute-start | bytes 55304 | tf_op jit(solution)/shard_map/ppermute | solution.py:1252
  213.2 13.7 %collective-permute-start.18 = (bf16[2,192,384]{2,1,0:T(8,128)(2,1)S(1)}, bf16[2,192,384]{2,1,0:T(8,128)(2,1)S(1)}, u32[]{:S(2)}, u32[]{:S(2)}) collective-permute-start(bf16[2,192,384]{2,1,0:T(8,128)(2,1)S(1)} %pad_maximum_fusion.2), channel_id=1, source_target_pairs={{0,8},{8,16},{16,24},{1,9},{9,17},{17,25},{2,10},{10,18},{18,26},{... | collective-permute-start | bytes 884744 | tf_op jit(solution)/shard_map/ppermute | solution.py:976
  217.1 13.2 %collective-permute-start.19 = (bf16[2,192,384]{2,1,0:T(8,128)(2,1)S(1)}, bf16[2,192,384]{2,1,0:T(8,128)(2,1)S(1)}, u32[]{:S(2)}, u32[]{:S(2)}) collective-permute-start(bf16[2,192,384]{2,1,0:T(8,128)(2,1)S(1)} %pad_maximum_fusion.3), channel_id=1, source_target_pairs={{8,0},{16,8},{24,16},{9,1},{17,9},{25,17},{10,2},{18,10},{26,18},{... | collective-permute-start | bytes 884744 | tf_op jit(solution)/shard_map/ppermute | solution.py:976
  (16 other events, 89.0 us)
